TPU v7x, 512 devices: a whole 4x8x8 slice. The times are simulated.
512 devices in a mesh: ctx: 32 (over z, x), tp: 16 (over y, core).
Axes of the slice: x: 4, y: 8, z: 8, core: 2. Of those that a mesh axis runs over, the one named last changes fastest.
Arguments:
- q_slab: bfloat16 [2048, 8192], P(('ctx', 'tp')), may hold values from -6 to 6, as said below
- k_cache: bfloat16 [16384, 1024], P('ctx'), may hold values from -6 to 6, as said below
- v_cache: bfloat16 [16384, 1024], P('ctx'), may hold values from -6 to 6
- out_weight: bfloat16 [8192, 8192], P('ctx', 'tp'), may hold values from -0.0625 to 0.0625
- pattern_type: int32 [64], replicated, may hold values 0 or 1
- block_count: int32 [64], replicated, may hold values from 1 to 16, as said below
- kv_blocks: int32 [64, 32, 16], replicated, may hold values from 0 to 255, as said below
- vertical_cols: int32 [64, 1024], replicated, may hold values from 0 to 13823, as said below
- slash_offsets: int32 [64, 128], replicated, may hold values from 0 to 511, as said below
Outputs:
- projected: bfloat16 [2048, 8192], P(('ctx', 'tp'))
Inputs may be any that keep to these rules, and one draw needn't show every extreme that they name: `q_slab`: entries are at most 6 in magnitude. `k_cache`: entries are at most 6 in magnitude. `block_count`: some head has 16 and some head has 1. kv_blocks[h, b, 0] is the query block's own key block (14336) / 64 + b; kv_blocks[h, b, 1] is key block 0; entries 1 to 15 of a row are distinct key blocks below the own one. `vertical_cols`: the columns of one head are distinct and include 0 and 13823. `slash_offsets`: the offsets of one head are distinct; its first two are 0 and 1, and 511 is among them.
All inputs are finite; a program needn't handle non-finite values.
Results may differ from a plain program's by a relative error of at most 0.02.
Values may be sent and summed in bfloat16 or wider, within the bound.
A program may use at most 64 MiB of HBM per device.

v0:
```python
import math

import jax
import jax.numpy as jnp
import numpy as np
from jax import lax
from jax.sharding import PartitionSpec as P

H = 64
KVH = 8
HD = 128
NSEL = 16
SMAX = 512
BLK = 64


masked_score = -1e30


def block_pattern(query_groups, group_positions, key_head, value_head, chosen, tile_count):
    groups, group_rows, _ = query_groups.shape
    score_scale = 1.0 / math.sqrt(HD)
    tiles_turn = 8
    span_width = tiles_turn * BLK
    turn_total = (NSEL + tiles_turn - 1) // tiles_turn
    slot_tile = jnp.arange(span_width, dtype=jnp.int32) // BLK
    slot_offset = jnp.arange(span_width, dtype=jnp.int32) % BLK
    turn_count = (tile_count + tiles_turn - 1) // tiles_turn

    def tile_places(turn_index):
        tile_index = turn_index * tiles_turn + slot_tile
        block_ids = jnp.take(chosen, jnp.minimum(tile_index, NSEL - 1), axis=1)
        key_index = block_ids * BLK + slot_offset[None, :]
        usable = (tile_index < tile_count)[None, None, :] & (
            key_index[:, None, :] <= group_positions[:, :, None]
        )
        return (key_index, usable)

    def score_turn(turn_index, score_buffer):
        key_index, usable = tile_places(turn_index)
        key_rows = key_head[key_index]
        scores = (
            jnp.einsum("gqd,gkd->gqk", query_groups, key_rows, preferred_element_type=jnp.float32)
            * score_scale
        )
        scores = jnp.where(usable, scores, masked_score)
        return lax.dynamic_update_slice_in_dim(score_buffer, scores, turn_index * span_width, 2)

    start_buffer = jnp.full(
        (groups, group_rows, turn_total * span_width), masked_score, jnp.float32
    )
    score_buffer = lax.fori_loop(0, turn_count, score_turn, start_buffer)
    row_max = jnp.max(score_buffer, axis=2)

    def accumulate(turn_index, loop_state):
        weight_total, mixed_sum = loop_state
        key_index, usable = tile_places(turn_index)
        scores = lax.dynamic_slice_in_dim(score_buffer, turn_index * span_width, span_width, 2)
        weights = jnp.where(usable, jnp.exp(scores - row_max[:, :, None]), 0.0)
        value_rows = value_head[key_index]
        mixed_sum = mixed_sum + jnp.einsum(
            "gqk,gkd->gqd",
            weights.astype(jnp.bfloat16),
            value_rows,
            preferred_element_type=jnp.float32,
        )
        return (weight_total + jnp.sum(weights, axis=2), mixed_sum)

    start_state = (
        jnp.zeros((groups, group_rows), jnp.float32),
        jnp.zeros((groups, group_rows, HD), jnp.float32),
    )
    weight_total, mixed_sum = lax.fori_loop(0, turn_count, accumulate, start_state)
    return (
        (mixed_sum / weight_total[:, :, None]).astype(jnp.bfloat16).reshape(groups * group_rows, HD)
    )


def slash_pattern(query_groups, group_positions, key_head, value_head, columns, offsets):
    groups, group_rows, _ = query_groups.shape
    score_scale = 1.0 / math.sqrt(HD)
    band_width = SMAX + group_rows
    band_start = group_positions[:, 0] - SMAX

    def take_band(start_row):
        return (
            lax.dynamic_slice_in_dim(key_head, start_row, band_width, 0),
            lax.dynamic_slice_in_dim(value_head, start_row, band_width, 0),
        )

    band_keys, band_values = jax.vmap(take_band)(band_start)
    distance = (
        jnp.arange(group_rows, dtype=jnp.int32)[:, None]
        + SMAX
        - jnp.arange(band_width, dtype=jnp.int32)[None, :]
    )
    on_diagonal = jnp.any(distance[:, :, None] == offsets[None, None, :], axis=2)
    column_keys = key_head[columns]
    column_values = value_head[columns]
    column_scores = (
        jnp.einsum("gqd,kd->gqk", query_groups, column_keys, preferred_element_type=jnp.float32)
        * score_scale
    )
    band_scores = (
        jnp.einsum("gqd,gkd->gqk", query_groups, band_keys, preferred_element_type=jnp.float32)
        * score_scale
    )
    band_scores = jnp.where(on_diagonal[None, :, :], band_scores, masked_score)
    row_max = jnp.maximum(jnp.max(column_scores, axis=2), jnp.max(band_scores, axis=2))[:, :, None]
    column_weights = jnp.exp(column_scores - row_max)
    band_weights = jnp.where(on_diagonal[None, :, :], jnp.exp(band_scores - row_max), 0.0)
    weight_total = jnp.sum(column_weights, axis=2, keepdims=True) + jnp.sum(
        band_weights, axis=2, keepdims=True
    )
    mixed_sum = jnp.einsum(
        "gqk,kd->gqd",
        column_weights.astype(jnp.bfloat16),
        column_values,
        preferred_element_type=jnp.float32,
    )
    mixed_sum = mixed_sum + jnp.einsum(
        "gqk,gkd->gqd",
        band_weights.astype(jnp.bfloat16),
        band_values,
        preferred_element_type=jnp.float32,
    )
    return (mixed_sum / weight_total).astype(jnp.bfloat16).reshape(groups * group_rows, HD)


def shards(
    q_slab,
    k_cache,
    v_cache,
    out_weight,
    pattern_type,
    block_count,
    kv_blocks,
    vertical_cols,
    slash_offsets,
):
    ctx_devices = lax.axis_size("ctx")
    tp_devices = lax.axis_size("tp")
    ctx_place = lax.axis_index("ctx")
    tp_place = lax.axis_index("tp")
    query_rows = q_slab.shape[0]
    shard_keys = k_cache.shape[0]
    heads_local = H // ctx_devices
    group_size = H // KVH
    context_length = shard_keys * ctx_devices
    slab_length = query_rows * ctx_devices * tp_devices
    slab_start = context_length - slab_length
    by_head = lax.all_to_all(q_slab, "ctx", split_axis=1, concat_axis=0, tiled=True)
    kv_target = np.arange(ctx_devices) * heads_local // group_size
    local_keys = k_cache.reshape(shard_keys, KVH, HD)
    local_values = v_cache.reshape(shard_keys, KVH, HD)
    key_head, value_head = (
        lax.all_to_all(local_keys[:, kv_target, :], "ctx", split_axis=1, concat_axis=0, tiled=True),
        lax.all_to_all(
            local_values[:, kv_target, :], "ctx", split_axis=1, concat_axis=0, tiled=True
        ),
    )
    key_head = key_head.reshape(context_length, HD)
    value_head = value_head.reshape(context_length, HD)
    row_blocks = jnp.arange(ctx_devices, dtype=jnp.int32) * tp_devices + tp_place
    group_positions = (
        slab_start
        + row_blocks[:, None] * query_rows
        + jnp.arange(query_rows, dtype=jnp.int32)[None, :]
    )
    group_block = row_blocks * query_rows // BLK
    head_outputs = []
    for local_head in range(heads_local):
        head_index = ctx_place * heads_local + local_head
        query_head = by_head[:, local_head * HD : (local_head + 1) * HD]
        chosen = jnp.take(kv_blocks[head_index], group_block, axis=0)
        tile_count = block_count[head_index]
        columns = vertical_cols[head_index]
        offsets = slash_offsets[head_index]
        query_groups = query_head.reshape(ctx_devices, query_rows, HD)
        head_result = lax.cond(
            pattern_type[head_index] == 0,
            lambda: block_pattern(
                query_groups, group_positions, key_head, value_head, chosen, tile_count
            ),
            lambda: slash_pattern(
                query_groups, group_positions, key_head, value_head, columns, offsets
            ),
        )
        head_outputs.append(head_result)
    attended = jnp.concatenate(head_outputs, axis=1)
    full_weight = lax.all_gather(out_weight, "tp", axis=1, tiled=True)
    return lax.psum_scatter(
        jnp.dot(attended, full_weight, preferred_element_type=jnp.float32).astype(jnp.bfloat16),
        "ctx",
        scatter_dimension=0,
        tiled=True,
    )


def solution(mesh):
    return jax.shard_map(
        shards,
        mesh=mesh,
        in_specs=(
            P(("ctx", "tp"), None),
            P("ctx", None),
            P("ctx", None),
            P("ctx", "tp"),
            P(),
            P(),
            P(),
            P(),
            P(),
        ),
        out_specs=P(("ctx", "tp"), None),
        check_vma=False,
    )
```

profile of v0, /device:TPU:1, one launch (start us, length us, event | category | flops | bytes accessed | tf_op | source)
XLA Modules:
  0.0 914.2 jit_solution(14736615660880862003)
XLA Ops:
  6.5 13.8 %all-to-all-start.1 = ((bf16[4,32,256]{2,0,1:T(4,128)(2,1)}), bf16[4,32,256]{2,0,1:T(4,128)(2,1)S(1)}, u32[]{:S(2)}, u32[]{:S(2)}) async-start(bf16[4,32,256]{2,0,1:T(4,128)(2,1)} %bitcast.221), calls=%async_computation.1 | async-start | bytes 131072 | tf_op jit(solution)/shard_map/all_to_all | solution.py:152
  25.7 3.6 all-to-all-done.1
  29.2 5.9 all-to-all-start
  39.4 87.8 %all-to-all-done = bf16[512,32,128]{2,0,1:T(8,128)(2,1)} async-done(((bf16[512,32,128]{2,0,1:T(8,128)(2,1)}), bf16[512,32,128]{2,0,1:T(8,128)(2,1)}, u32[]{:S(2)}, u32[]{:S(2)}) %all-to-all-start) | async-done | bytes 4194336 | tf_op jit(solution)/shard_map/all_to_all | solution.py:157
  127.2 8.8 all-to-all-start.2
  140.8 87.3 %all-to-all-done.2 = bf16[512,32,128]{2,0,1:T(8,128)(2,1)} async-done(((bf16[512,32,128]{2,0,1:T(8,128)(2,1)}), bf16[512,32,128]{2,0,1:T(8,128)(2,1)}, u32[]{:S(2)}, u32[]{:S(2)}) %all-to-all-start.2) | async-done | bytes 4194336 | tf_op jit(solution)/shard_map/all_to_all | solution.py:158
  228.2 256.2 %conditional.2 = (bf16[128,128]{1,0:T(8,128)(2,1)S(1)}) conditional(s32[]{:T(128)} %bitcast.20, (s32[64,1024]{1,0:T(8,128)}, s32[]{:T(128)}, bf16[16384,128]{1,0:T(8,128)(2,1)}, bf16[32,4,128]{2,1,0:T(4,128)(2,1)S(1)}, s32[64,128]{1,0:T(8,128)}, /*index=5*/s32[32,4]{1,0:T(8,128)S(1)}, bf16[16384,128]{1,0:T(8,128)(2,1)}) %tuple.229, ...), branch_computations={%region_0.7_spmd, %region_6.15_spmd} | conditional | flops 102887816 | bytes 29452120 | solution.py:180
  229.5 127.2 %while.52 = (s32[]{:T(128)}, f32[32,4,1024]{2,1,0:T(4,128)S(1)}, s32[]{:T(128)}, s32[]{:T(128)}, s32[32,16]{0,1:T(8,128)S(1)}, /*index=5*/s32[32,4]{1,0:T(8,128)...) while((s32[]{:T(128)}, f32[32,4,1024]{2,1,0:T(4,128)S(1)}, ...), condition=%wide.region_8.10_spmd.clone, body=%wide.region_7.9_spmd.clone.sunk | while | flops 17173512 | bytes 13893831 | solution.py:52
  231.6 58.0 %gather_fusion.7 = bf16[16384,128]{1,0:T(8,128)(2,1)} fusion(bf16[16384,128]{1,0:T(8,128)(2,1)} %get-tuple-element.1337, s32[16384]{0:T(1024)S(1)} %broadcast_clamp_fusion.12), kind=kCustom, calls=%fused_computation.2.clone.clone.1 | custom fusion | bytes 8454144 | tf_op jit(solution)/shard_map/cond/branch_1_fun/while/body/gather | solution.py:41
  289.7 3.4 fusion.160
  295.2 58.0 %gather_fusion.7 = bf16[16384,128]{1,0:T(8,128)(2,1)} fusion(bf16[16384,128]{1,0:T(8,128)(2,1)} %get-tuple-element.1337, s32[16384]{0:T(1024)S(1)} %broadcast_clamp_fusion.12), kind=kCustom, calls=%fused_computation.2.clone.clone.1 | custom fusion | bytes 8454144 | tf_op jit(solution)/shard_map/cond/branch_1_fun/while/body/gather | solution.py:41
  353.3 3.4 fusion.160
  356.9 127.0 %while.53 = (s32[]{:T(128)}, f32[32,4]{1,0:T(8,128)S(1)}, f32[32,4,128]{2,1,0:T(4,128)S(1)}, s32[]{:T(128)}, s32[]{:T(128)}, /*index=5*/s32[32,16]{0,1:T(8,128)S...) while((s32[]{:T(128)}, f32[32,4]{1,0:T(8,128)S(1)}, ...), condition=%wide.region_12.14_spmd.clone, body=%wide.region_10.13_spmd.clone.sunk | while | flops 17583112 | bytes 14339803 | solution.py:73
  359.0 58.0 %gather_fusion.9 = bf16[16384,128]{1,0:T(8,128)(2,1)} fusion(bf16[16384,128]{1,0:T(8,128)(2,1)} %get-tuple-element.1383, s32[16384]{0:T(1024)S(1)} %broadcast_clamp_fusion.13), kind=kCustom, calls=%fused_computation.9.clone.clone.1 | custom fusion | bytes 8454144 | tf_op jit(solution)/shard_map/cond/branch_1_fun/while/body/gather | solution.py:60
  422.5 58.0 %gather_fusion.9 = bf16[16384,128]{1,0:T(8,128)(2,1)} fusion(bf16[16384,128]{1,0:T(8,128)(2,1)} %get-tuple-element.1383, s32[16384]{0:T(1024)S(1)} %broadcast_clamp_fusion.13), kind=kCustom, calls=%fused_computation.9.clone.clone.1 | custom fusion | bytes 8454144 | tf_op jit(solution)/shard_map/cond/branch_1_fun/while/body/gather | solution.py:60
  484.3 209.6 %conditional.3 = (bf16[128,128]{1,0:T(8,128)(2,1)S(1)}) conditional(s32[]{:T(128)} %bitcast.39, (s32[64,1024]{1,0:T(8,128)}, s32[]{:T(128)}, bf16[16384,128]{1,0:T(8,128)(2,1)}, bf16[32,4,128]{2,1,0:T(4,128)(2,1)S(1)}, s32[64,128]{1,0:T(8,128)}, /*index=5*/s32[32,4]{1,0:T(8,128)S(1)}, bf16[16384,128]{1,0:T(8,128)(2,1)}) %tuple.227, ...), branch_computations={%region_13.21_spmd, %region_19.28_spmd} | conditional | flops 102887816 | bytes 29452120 | solution.py:180
  485.1 10.7 %compare_reduce_fusion.1 = pred[4,516]{0,1:T(8,128)(4,1)S(1)} fusion(s32[128]{0:T(128)S(1)} %dynamic-slice_bitcast_fusion.1, s32[4,516]{0,1:T(8,128)S(1)} %iota_subtract_fusion.1), kind=kLoop, calls=%fused_computation.70 | loop fusion | flops 526320 | bytes 10832 | tf_op jit(solution)/shard_map/cond/branch_0_fun/reduce_or | solution.py:97
  498.5 86.5 %while.50 = (s32[]{:T(128)}, bf16[16384,128]{1,0:T(8,128)(2,1)}, s32[32,2]{0,1:T(2,128)S(1)}, bf16[32,516,128]{2,1,0:T(8,128)(2,1)}, s32[]{:T(128)}) while((s32[]{:T(128)}, bf16[16384,128]{1,0:T(8,128)(2,1)}, s32[32,2]{0,1:T(2,128)S(1)}, bf16[32,516,128]{2,1,0:T(8,128)(2,1)}, s32[]{:T(128)}) %tuple.197), condition=%wide.while_cond.2, body=%wide.while_body.2.sunk | while | flops 2 | bytes 267353 | solution.py:87
  585.0 3.5 fusion.117
  589.4 5.6 gather_fusion.4
  598.5 86.5 %while.51 = (s32[]{:T(128)}, bf16[16384,128]{1,0:T(8,128)(2,1)}, s32[32,2]{0,1:T(2,128)S(1)}, bf16[32,516,128]{2,1,0:T(8,128)(2,1)}, s32[]{:T(128)}) while((s32[]{:T(128)}, bf16[16384,128]{1,0:T(8,128)(2,1)}, s32[32,2]{0,1:T(2,128)S(1)}, bf16[32,516,128]{2,1,0:T(8,128)(2,1)}, s32[]{:T(128)}) %tuple.232), condition=%wide.while_cond.3, body=%wide.while_body.3.sunk | while | flops 2 | bytes 267353 | solution.py:88
  688.0 5.6 gather_fusion.5
  694.0 4.3 convolution_convert_fusion
  700.2 205.6 %all-reduce.5.cloned.1.call-done = bf16[128,8192]{1,0:T(8,128)(2,1)} async-done(((bf16[128,8192]{1,0:T(8,128)(2,1)}), bf16[128,8192]{1,0:T(8,128)(2,1)}) %all-reduce.5.cloned.1.call-update) | async-done | bytes 2097168
  (305 shorter events, 215.8 us)
Async XLA Ops:
  6.5 16.0 %copy-start.3 = (s32[32]{0:T(128)S(1)}, s32[32]{0:T(128)}, u32[]{:S(2)}) copy-start(s32[32]{0:T(128)} %constant.419) | copy-start | bytes 388
  6.5 22.7 %all-to-all-start.1 = ((bf16[4,32,256]{2,0,1:T(4,128)(2,1)}), bf16[4,32,256]{2,0,1:T(4,128)(2,1)S(1)}, u32[]{:S(2)}, u32[]{:S(2)}) async-start(bf16[4,32,256]{2,0,1:T(4,128)(2,1)} %bitcast.221), calls=%async_computation.1 | async-start | bytes 131072 | tf_op jit(solution)/shard_map/all_to_all | solution.py:152
  29.2 5.9 copy-start.1
  29.2 97.9 %all-to-all-start = ((bf16[512,32,128]{2,0,1:T(8,128)(2,1)}), bf16[512,32,128]{2,0,1:T(8,128)(2,1)}, u32[]{:S(2)}, u32[]{:S(2)}) async-start(bf16[512,32,128]{2,0,1:T(8,128)(2,1)} %bitcast.199), calls=%async_computation | async-start | bytes 8388608 | tf_op jit(solution)/shard_map/all_to_all | solution.py:157
  127.1 9.6 %copy-start = (s32[64,32,16]{0,2,1:T(8,128)S(1)}, s32[64,32,16]{0,2,1:T(8,128)}, u32[]{:S(2)}) copy-start(s32[64,32,16]{0,2,1:T(8,128)} %param.34) | copy-start | bytes 393220
  127.1 11.5 %copy-start.2 = (s32[64]{0:T(128)S(1)}, s32[64]{0:T(128)}, u32[]{:S(2)}) copy-start(s32[64]{0:T(128)} %param.32) | copy-start | bytes 772
  127.1 101.0 %copy-start.4 = (s32[64]{0:T(128)S(1)}, s32[64]{0:T(128)}, u32[]{:S(2)}) copy-start(s32[64]{0:T(128)} %param.33) | copy-start | bytes 772
  127.2 101.0 %all-to-all-start.2 = ((bf16[512,32,128]{2,0,1:T(8,128)(2,1)}), bf16[512,32,128]{2,0,1:T(8,128)(2,1)}, u32[]{:S(2)}, u32[]{:S(2)}) async-start(bf16[512,32,128]{2,0,1:T(8,128)(2,1)} %bitcast.198), calls=%async_computation.2 | async-start | bytes 8388608 | tf_op jit(solution)/shard_map/all_to_all | solution.py:158
  135.9 558.0 %all-gather.2.cloned.1.call-start = ((), (), s32[]{:S(2)}) async-start(), calls=%async_computation.3 | async-start | bytes 4456448 | tf_op jit(solution)/shard_map/all_gather | solution.py:191
  136.7 769.1 %all-reduce.5.cloned.1.call-start = ((), (), s32[]{:S(2)}) async-start(), calls=%async_computation.4 | async-start | bytes 4194304
Sparse Core Ops, SparseCore 0:
  138.9 46.6 all-gather.1
  698.4 207.3 all-reduce.4
where the time goes:
time: 920 us; the launch traced here: 914 us
  local copies, waits for them, and re-layouts  443 us (48%)
  waiting for transfers between devices  385 us (42%)
  starting transfers between devices  28.6 us (3%)
  matrix products  24.2 us (3%)
  other arithmetic  16.4 us (2%)
  between operations  15.5 us (2%)
    unnamed x3, waiting for transfers between devices  206 us
    gather x192, local copies, waits for them, and re-layouts  173 us
    gather x2, local copies, waits for them, and re-layouts, score_turn(): key_rows = key_head[key_index]  116 us
    gather x2, local copies, waits for them, and re-layouts, accumulate(): value_rows = value_head[key_index]  116 us
    all_to_all x1, waiting for transfers between devices, shards(): lax.all_to_all(local_keys[:, kv_target, :], 'ctx', split_axis=1, concat_a...  87.8 us
    all_to_all x1, waiting for transfers between devices, shards(): lax.all_to_all(local_values[:, kv_target, :], 'ctx', split_axis=1, concat...  87.3 us
  transfers between devices with their start and end apart: 5, of which 4 were waited for; matrix products, arithmetic and copies ran while one was open for 52% of the time, Pallas kernels for 0%

commit v1 on v0

v1 whole, which is shorter than its diff:
```python
import math

import jax
import jax.numpy as jnp
from jax import lax
from jax.experimental import pallas as pl
from jax.experimental.pallas import tpu as pltpu
from jax.sharding import PartitionSpec as P

H = 64
KVH = 8
HD = 128
BLK = 64
SLAB0 = 14336
NX, NZ, NY = 4, 8, 8
NT = 2 * NY
PART = 4096
MASKED = -1e30
MESH = pl.DeviceIdType.MESH
VMEM_LIMIT = 48 * 1024 * 1024
F32 = jnp.float32
BF16 = jnp.bfloat16


def place():
    ctx = lax.axis_index("ctx")
    tp = lax.axis_index("tp")
    return ctx, tp, ctx // NX, ctx % NX, tp // 2, tp % 2


def remote(src, dst, send_sem, recv_sem, ctx, tp):
    return pltpu.make_async_remote_copy(
        src_ref=src,
        dst_ref=dst,
        send_sem=send_sem,
        recv_sem=recv_sem,
        device_id=(ctx, tp),
        device_id_type=MESH,
    )


def arrived(ref, sem):
    pltpu.make_async_copy(ref, ref, sem).wait()


def ring_gather(view, ctx, y, c, sends, right_recv, left_recv, on_arrival):
    right = ((y + 1) % NY) * 2 + c
    left = ((y + NY - 1) % NY) * 2 + c
    started = []
    for s in range(4):
        from_left = (y + NY - s) % NY
        from_right = (y + s) % NY
        for h in range(2):
            here_r = view(from_left, h)
            here_l = view(from_right, h)
            if s > 0:
                arrived(here_r, right_recv.at[2 * (s - 1) + h])
                on_arrival(here_r)
            if s < 3 or h == 0:
                copy = remote(here_r, here_r, sends.at[4 * s + h], right_recv.at[2 * s + h], ctx, right)
                copy.start()
                started.append(copy)
            if s > 0:
                arrived(here_l, left_recv.at[2 * (s - 1) + h])
                on_arrival(here_l)
            if s < 3 or h == 1:
                copy = remote(here_l, here_l, sends.at[4 * s + 2 + h], left_recv.at[2 * s + h], ctx, left)
                copy.start()
                started.append(copy)
    across = (y + 4) % NY
    for h in range(2):
        ref = view(across, h)
        arrived(ref, (right_recv if h == 0 else left_recv).at[6 + h])
        on_arrival(ref)
    return started


def spread_kernel(
    q_ref, k_ref, v_ref, w_ref,
    qb, kvb, wb,
    qt, qs, q2, qf,
    q1_send, q1_recv, q2_send, q2_recv, qx_send, qx_recv,
    kz_send, kz_recv, ring_send, right_recv, left_recv, core_send, core_recv,
    w_send, w_recv, wc_send, wc_recv, local_sem,
):
    ctx, t, z, x, y, c = place()
    zc = z // 4
    partner = 2 * y + 1 - c

    barrier = pltpu.get_barrier_semaphore()
    for d in range(1, NT):
        pl.semaphore_signal(barrier, inc=1, device_id=(ctx, (t + d) % NT), device_id_type=MESH)
    for d in range(1, NZ):
        pl.semaphore_signal(barrier, inc=1, device_id=(((z + d) % NZ) * NX + x, t), device_id_type=MESH)
    for d in range(1, NX):
        pl.semaphore_signal(barrier, inc=1, device_id=(z * NX + (x + d) % NX, t), device_id_type=MESH)

    for yy in range(NY):
        for g in range(KVH):
            head = 8 * g + yy
            qt[yy, g] = q_ref[:, head * HD : (head + 1) * HD].astype(F32)

    pl.semaphore_wait(barrier, NT - 1 + NZ - 1 + NX - 1)

    q1 = [
        remote(qt.at[(y + d) % NY], qs.at[t], q1_send.at[d], q1_recv, ctx, ((y + d) % NY) * 2 + zc)
        for d in range(NY)
    ]
    for d in range(1, NY):
        q1[d].start()

    @pl.when(zc == c)
    def _():
        pltpu.make_async_copy(qt.at[y], qs.at[t], q1_recv).start()

    @pl.when(zc != c)
    def _():
        q1[0].start()

    rows = pl.ds(pl.multiple_of(32 * t, 32), 32)
    kz = []
    for d in (4, 3, 5, 2, 6, 1, 7):
        g = (z + d) % NZ
        cols = pl.ds(pl.multiple_of(HD * g, HD), HD)
        for i, ref in enumerate((k_ref, v_ref)):
            copy = remote(ref.at[rows, cols], kvb.at[t, i, z], kz_send.at[2 * d + i], kz_recv, g * NX + x, t)
            copy.start()
            kz.append(copy)
    own = pl.ds(pl.multiple_of(HD * z, HD), HD)
    for i, ref in enumerate((k_ref, v_ref)):
        pltpu.make_async_copy(ref.at[rows, own], kvb.at[t, i, z], kz_recv).start()

    def w_view(xx, cc):
        return wb.at[
            pl.ds(pl.multiple_of(256 * xx, 256), 256), pl.ds(pl.multiple_of(512 * cc, 512), 512)
        ]

    wx = [
        remote(w_ref, w_view(x, c), w_send.at[d], w_recv.at[d], z * NX + (x + d) % NX, t)
        for d in range(1, NX)
    ]
    for copy in wx:
        copy.start()
    w_own = pltpu.make_async_copy(w_ref, w_view(x, c), local_sem)
    w_own.start()
    wc = [remote(w_ref, w_view(x, c), wc_send.at[0], wc_recv, ctx, partner)]
    wc[0].start()

    @pl.when(zc == c)
    def _():
        arrived(qs, q1_recv)
        for d in range(1, NZ):
            g = (z + d) % NZ
            remote(qs.at[:, g], q2.at[z % 4], q2_send.at[d], q2_recv, g * NX + x, t).start()
        pltpu.make_async_copy(qs.at[:, z], q2.at[z % 4], q2_recv).start()

    arrived(kvb.at[t], kz_recv)
    to_core = []

    def on_core(ref):
        copy = remote(ref, ref, core_send.at[len(to_core)], core_recv, ctx, partner)
        copy.start()
        to_core.append(copy)

    for h in range(2):
        on_core(kvb.at[t, h])

    arrived(q2, q2_recv)
    for i in range(64):
        qf[4 * i : 4 * i + 4, :] = q2[i // 16, i % 16]
    qb[x] = qf[...].astype(BF16)
    qx = [
        remote(qb.at[x], qb.at[x], qx_send.at[d], qx_recv.at[d], z * NX + (x + d) % NX, t)
        for d in range(1, NX)
    ]
    for copy in qx:
        copy.start()

    ring = ring_gather(
        lambda yy, h: kvb.at[2 * yy + c, h], ctx, y, c, ring_send, right_recv, left_recv, on_core
    )

    for d in range(1, NX):
        xx = (x + NX - d) % NX
        ref = w_view(xx, c)
        arrived(ref, w_recv.at[d])
        copy = remote(ref, ref, wc_send.at[d], wc_recv, ctx, partner)
        copy.start()
        wc.append(copy)
    for d in range(1, NX):
        arrived(qb.at[(x + NX - d) % NX], qx_recv.at[d])
    arrived(kvb.at[pl.ds(0, NY)], core_recv)
    arrived(wb.at[:, pl.ds(0, 512)], wc_recv)
    w_own.wait()
    for copy in q1[1:] + kz + wx + wc + qx + ring + to_core:
        copy.wait_send()

    @pl.when(zc != c)
    def _():
        q1[0].wait_send()

    @pl.when(zc == c)
    def _():
        for d in range(1, NZ):
            g = (z + d) % NZ
            remote(qs.at[:, g], q2.at[z % 4], q2_send.at[d], q2_recv, g * NX + x, t).wait_send()


def spread(q, k, v, w):
    dma = pltpu.SemaphoreType.DMA
    any_spec = pl.BlockSpec(memory_space=pl.ANY)
    vmem = pl.BlockSpec(memory_space=pltpu.VMEM)
    return pl.pallas_call(
        spread_kernel,
        out_shape=(
            jax.ShapeDtypeStruct((NX, 256, HD), BF16),
            jax.ShapeDtypeStruct((NT, 2, NZ, 32, HD), BF16),
            jax.ShapeDtypeStruct((1024, 1024), BF16),
        ),
        in_specs=[vmem, any_spec, any_spec, any_spec],
        out_specs=(vmem, vmem, any_spec),
        scratch_shapes=[
            pltpu.VMEM((NY, KVH, 4, HD), F32),
            pltpu.VMEM((NT, KVH, 4, HD), F32),
            pltpu.VMEM((4, NT, 4, HD), F32),
            pltpu.VMEM((256, HD), F32),
            dma((8,)), dma, dma((8,)), dma, dma((4,)), dma((4,)),
            dma((16,)), dma, dma((16,)), dma((8,)), dma((8,)), dma((16,)), dma,
            dma((4,)), dma((4,)), dma((4,)), dma, dma,
        ],
        compiler_params=pltpu.CompilerParams(
            collective_id=0, has_side_effects=True, vmem_limit_bytes=VMEM_LIMIT
        ),
        name="spread",
    )(q, k, v, w)


def attend_kernel(
    kind_ref, count_ref, blocks_ref, cols_ref, offs_ref, qb, kvb,
    o_ref, st_ref,
    row_bias, tile_bias, scores,
):
    ctx, t, z, x, y, c = place()
    head = 8 * z + y
    slash = kind_ref[head] == 1
    count = count_ref[head]

    def lanes(shape):
        return lax.broadcasted_iota(jnp.int32, shape, len(shape) - 1)

    def subs(shape):
        return lax.broadcasted_iota(jnp.int32, shape, 0)

    @pl.when(slash)
    def _():
        cols = cols_ref[pl.ds(head, 1), :]
        tile = subs((32, 1024))
        tile = 16 * (tile // 4) + 4 * x + tile % 4
        hi = jnp.where(cols // 128 == tile, 1.0, 0.0).astype(BF16)
        lo = jnp.where(cols % 128 == subs((128, 1024)), 1.0, 0.0).astype(BF16)
        member = lax.dot_general(hi, lo, (((1,), (1,)), ((), ())), preferred_element_type=F32)
        bias = jnp.where(member > 0.5, 0.0, MASKED)
        for i in range(32):
            row_bias[i] = jnp.broadcast_to(bias[i : i + 1, :], (32, 128))
        rev = 511 - offs_ref[pl.ds(head, 1), :]
        lo_row = subs((128, 128))
        hi_row = subs((8, 128))
        rows = []
        for phase in range(2):
            place_of = rev + 128 + 64 * phase
            hi = jnp.where(place_of // 128 == hi_row, 1.0, 0.0).astype(BF16)
            lo = jnp.where(place_of % 128 == lo_row, 1.0, 0.0).astype(BF16)
            found = lax.dot_general(hi, lo, (((1,), (1,)), ((), ())), preferred_element_type=F32)
            rows.append(jnp.where(found > 0.5, 0.0, MASKED))
        tile_bias[0] = jnp.full((64, 128), MASKED, F32)
        tile_bias[11] = jnp.full((64, 128), MASKED, F32)
        for i in range(10):
            start = 448 - 64 * i + 128
            phase = (start // 64) % 2
            first = (start + 64 * phase) // 128
            pair = jnp.concatenate(
                [rows[phase][first : first + 1, :], rows[phase][first + 1 : first + 2, :]], axis=1
            )
            wide = jnp.broadcast_to(pair, (64, 256))
            rolled = pltpu.roll(wide, 256 - 63, 1, stride=1, stride_axis=0)
            tile_bias[i + 1] = rolled[:, :128]

    @pl.when(jnp.logical_not(slash))
    def _():
        chosen = blocks_ref[head]
        place_of = lanes((32, 128))
        block = 8 * (4 * (place_of // 8) + x) + place_of % 8
        found = jnp.full((32, 128), MASKED, F32)
        for k in range(16):
            hit = jnp.logical_and(chosen[:, k : k + 1] == block, k < count)
            found = jnp.where(hit, 0.0, found)
        left = lanes((32, 128)) < 64
        for i in range(32):
            row_bias[i] = jnp.where(left, found[:, 2 * i : 2 * i + 1], found[:, 2 * i + 1 : 2 * i + 2])
        back = subs((64, 128)) - lanes((64, 128))
        for i in range(12):
            tile_bias[i] = jnp.where(back + 64 * (i - 1) >= 0, 0.0, MASKED)

    scale = math.log2(math.e) / math.sqrt(HD)

    def group(xx, carry):
        q = qb[xx]
        highest = [jnp.full((64, 128), -3e38, F32) for _ in range(4)]
        for zz in range(NZ):
            keys = kvb[:, 0, zz].reshape(512, HD)
            s = lax.dot_general(q, keys, (((1,), (1,)), ((), ())), preferred_element_type=F32)
            for zl in range(4):
                b = 16 * c + 4 * zl + xx
                for w in range(4):
                    bias = row_bias[4 * zz + w, pl.ds(b, 1), :]
                    if zz >= 6:
                        which = 224 + b - 8 * (4 * zz + x) - 2 * w + 1
                        band = tile_bias[jnp.clip(which, 0, 11)]
                        bias = jnp.where(slash, jnp.maximum(bias, band), jnp.minimum(bias, band))
                    part = s[64 * zl : 64 * zl + 64, 128 * w : 128 * w + 128] * scale + bias
                    scores[64 * zl : 64 * zl + 64, 512 * zz + 128 * w : 512 * zz + 128 * w + 128] = part
                    highest[zl] = jnp.maximum(highest[zl], part)
        top = [jnp.max(h, axis=1, keepdims=True) for h in highest]
        top = jnp.concatenate(top, axis=0)
        total = jnp.zeros((256, 128), F32)
        mixed = jnp.zeros((256, HD), F32)
        for zz in range(NZ):
            values = kvb[:, 1, zz].reshape(512, HD)
            weight = jnp.exp2(scores[:, 512 * zz : 512 * zz + 512] - top)
            for w in range(4):
                total = total + weight[:, 128 * w : 128 * w + 128]
            mixed = mixed + jnp.dot(weight.astype(BF16), values, preferred_element_type=F32)
        total = jnp.sum(total, axis=1, keepdims=True)
        o_ref[xx] = (mixed / total).astype(BF16)
        level = jnp.broadcast_to(top + jnp.log2(total), (256, 128))
        st_ref[xx] = level.T[:8, :]
        return carry

    lax.fori_loop(0, NX, group, 0)


def attend(kinds, counts, blocks, cols, offs, qb, kvb):
    vmem = pl.BlockSpec(memory_space=pltpu.VMEM)
    smem = pl.BlockSpec(memory_space=pltpu.SMEM)
    return pl.pallas_call(
        attend_kernel,
        out_shape=(
            jax.ShapeDtypeStruct((NX, 256, HD), BF16),
            jax.ShapeDtypeStruct((NX, 8, 256), F32),
        ),
        in_specs=[smem, smem, vmem, vmem, vmem, vmem, vmem],
        out_specs=(vmem, vmem),
        scratch_shapes=[
            pltpu.VMEM((32, 32, 128), F32),
            pltpu.VMEM((12, 64, 128), F32),
            pltpu.VMEM((256, PART), F32),
        ],
        compiler_params=pltpu.CompilerParams(vmem_limit_bytes=VMEM_LIMIT),
        name="attend",
    )(kinds, counts, blocks, cols, offs, qb, kvb)


def project_kernel(
    o_ref, st_ref, w_ref,
    out_ref,
    ob, sb, wv, ab, part, rb, fb, fr,
    ox_send, ox_recv, ring_send, right_recv, left_recv,
    z_send, z_recv, f_send, f_recv, w_sem,
):
    ctx, t, z, x, y, c = place()
    zc = z // 4

    w_copy = pltpu.make_async_copy(w_ref, wv, w_sem)
    w_copy.start()
    barrier = pltpu.get_barrier_semaphore()
    for d in range(1, NT):
        pl.semaphore_signal(barrier, inc=1, device_id=(ctx, (t + d) % NT), device_id_type=MESH)
    for d in range(1, NZ):
        for cc in range(2):
            pl.semaphore_signal(
                barrier, inc=1, device_id=(((z + d) % NZ) * NX + x, 2 * y + cc), device_id_type=MESH
            )
    for d in range(1, NX):
        pl.semaphore_signal(barrier, inc=1, device_id=(z * NX + (x + d) % NX, t), device_id_type=MESH)
    pl.semaphore_wait(barrier, NT - 1 + 2 * (NZ - 1) + NX - 1)

    sends = []
    for d in (2, 1, 3):
        xx = (x + d) % NX
        for i, (src, dst) in enumerate(((st_ref, sb), (o_ref, ob))):
            copy = remote(src.at[xx], dst.at[d], ox_send.at[2 * d + i], ox_recv.at[2 * d + i], z * NX + xx, t)
            copy.start()
            sends.append(copy)
    for d in range(1, NX):
        arrived(sb.at[d], ox_recv.at[2 * d])
    levels = [st_ref[x]] + [sb[d] for d in range(1, NX)]
    top = jnp.maximum(jnp.maximum(levels[0], levels[1]), jnp.maximum(levels[2], levels[3]))
    shares = [jnp.exp2(level - top) for level in levels]
    total = (shares[0] + shares[1]) + (shares[2] + shares[3])
    shares = [share / total for share in shares]
    table = jnp.concatenate(shares + [jnp.zeros((96, 256), F32)], axis=0).T
    for d in range(1, NX):
        arrived(ob.at[d], ox_recv.at[2 * d + 1])
    mixed = table[:, 0:1] * o_ref[x].astype(F32)
    for d in range(1, NX):
        mixed = mixed + table[:, 8 * d : 8 * d + 1] * ob[d].astype(F32)

    def view(yy, h):
        return ab.at[pl.ds(128 * h, 128), pl.ds(pl.multiple_of(HD * yy, HD), HD)]

    ab[:, pl.ds(pl.multiple_of(HD * y, HD), HD)] = mixed.astype(BF16)
    sends += ring_gather(view, ctx, y, c, ring_send, right_recv, left_recv, lambda ref: None)
    w_copy.wait()

    to_z = []
    for i in range(4):
        rows = jnp.dot(ab[64 * i : 64 * i + 64, :], wv[...], preferred_element_type=F32).astype(BF16)
        for cc in range(2):
            part[i, cc] = rows[:, 512 * cc : 512 * cc + 512]
    for i in range(4):
        zz = 4 * c + i
        for cc in range(2):
            copy = remote(part.at[i, cc], rb.at[z], z_send.at[2 * i + cc], z_recv, zz * NX + x, 2 * y + cc)
            to_z.append((zz, cc, i, copy))
            mine = jnp.logical_and(zz == z, cc == c)

            @pl.when(jnp.logical_not(mine))
            def _():
                copy.start()

            @pl.when(mine)
            def _():
                pltpu.make_async_copy(part.at[i, cc], rb.at[z], z_recv).start()

    arrived(rb, z_recv)
    summed = rb[0].astype(F32)
    for g in range(1, NZ):
        summed = summed + rb[g].astype(F32)
    for tt in range(NT):
        fb[tt] = summed[4 * tt : 4 * tt + 4, :]
    for d in range(1, NT):
        tt = (t + d) % NT
        copy = remote(fb.at[tt], fr.at[t], f_send.at[d], f_recv, ctx, tt)
        copy.start()
        sends.append(copy)
    pltpu.make_async_copy(fb.at[t], fr.at[t], f_recv).start()
    arrived(fr, f_recv)
    for tt in range(NT):
        out_ref[:, 512 * tt : 512 * tt + 512] = fr[tt].astype(BF16)
    for copy in sends:
        copy.wait_send()
    for zz, cc, i, copy in to_z:
        mine = jnp.logical_and(zz == z, cc == c)

        @pl.when(jnp.logical_not(mine))
        def _():
            copy.wait_send()


def project(o, st, w):
    dma = pltpu.SemaphoreType.DMA
    any_spec = pl.BlockSpec(memory_space=pl.ANY)
    vmem = pl.BlockSpec(memory_space=pltpu.VMEM)
    return pl.pallas_call(
        project_kernel,
        out_shape=jax.ShapeDtypeStruct((4, 8192), BF16),
        in_specs=[vmem, vmem, any_spec],
        out_specs=vmem,
        scratch_shapes=[
            pltpu.VMEM((NX, 256, HD), BF16),
            pltpu.VMEM((NX, 8, 256), F32),
            pltpu.VMEM((1024, 1024), BF16),
            pltpu.VMEM((256, 1024), BF16),
            pltpu.VMEM((4, 2, 64, 512), BF16),
            pltpu.VMEM((NZ, 64, 512), BF16),
            pltpu.VMEM((NT, 4, 512), F32),
            pltpu.VMEM((NT, 4, 512), F32),
            dma((8,)), dma((8,)), dma((16,)), dma((8,)), dma((8,)),
            dma((8,)), dma, dma((16,)), dma, dma,
        ],
        compiler_params=pltpu.CompilerParams(
            collective_id=1, has_side_effects=True, vmem_limit_bytes=VMEM_LIMIT
        ),
        name="project",
    )(o, st, w)


def shards(q, k, v, w, kinds, counts, blocks, cols, offs):
    qb, kvb, wb = spread(q, k, v, w)
    o, st = attend(kinds, counts, blocks, cols, offs, qb, kvb)
    return project(o, st, wb)


def solution(mesh):
    return jax.shard_map(
        shards,
        mesh=mesh,
        in_specs=(
            P(("ctx", "tp"), None),
            P("ctx", None),
            P("ctx", None),
            P("ctx", "tp"),
            P(),
            P(),
            P(),
            P(),
            P(),
        ),
        out_specs=P(("ctx", "tp"), None),
        check_vma=False,
    )
```

time: 920 us -> 107 us (0.12)
  local copies, waits for them, and re-layouts: 443 us -> 6.8 us
  waiting for transfers between devices: 385 us -> 0 us
  Pallas kernels: 0 us -> 98.7 us
  starting transfers between devices: 28.6 us -> 0 us
  matrix products: 24.2 us -> 0 us
  other arithmetic: 16.4 us -> 0 us
  between operations: 15.5 us -> 0.1 us
    gather x206 -> x0, local copies, waits for them, and re-layouts: 428 us -> none
    unnamed x3 -> x0, waiting for transfers between devices: 206 us -> none
    all_to_all x3 -> x0, waiting for transfers between devices: 179 us -> none  [the longest x1 87.8 us: shards(): lax.all_to_all(local_keys[:, kv_target, :], 'ctx', split_axis=1, concat_a...]
    pallas_call x0 -> x3, Pallas kernels: none -> 98.7 us  [the longest x1 45.1 us: spread(): pl.pallas_call(spread_kernel, out_shape=(jax.ShapeDtypeStruct((NX, 256, H...]
    all_to_all x3 -> x0, starting transfers between devices: 28.5 us -> none  [the longest x1 13.8 us: shards(): lax.all_to_all(q_slab, 'ctx', split_axis=1, concat_axis=0, tiled=True)]
    dot_general x9 -> x0, matrix products: 24.2 us -> none  [the longest x2 6.89 us: score_turn(): jnp.einsum('gqd,gkd->gqk', query_groups, key_rows, preferred_element_type...]
    reduce_or x1 -> x0, other arithmetic: 10.7 us -> none  [slash_pattern(): jnp.any(distance[:, :, None] == offsets[None, None, :], axis=2)]
  transfers between devices with their start and end apart: 5 -> 0, of which waited for: 4 -> 0; matrix products, arithmetic and copies ran while one was open for 52% -> 0% of each run, Pallas kernels for 0% -> 0%
where the time goes in v1:
time: 107 us; the launch traced here: 106 us
  Pallas kernels  98.7 us (92%)
  local copies, waits for them, and re-layouts  6.8 us (6%)
    pallas_call x1, Pallas kernels, spread(): pl.pallas_call(spread_kernel, out_shape=(jax.ShapeDtypeStruct((NX, 256, H...  45.1 us
    pallas_call x1, Pallas kernels, project(): pl.pallas_call(project_kernel, out_shape=jax.ShapeDtypeStruct((4, 8192),...  43.7 us
    pallas_call x1, Pallas kernels, attend(): pl.pallas_call(attend_kernel, out_shape=(jax.ShapeDtypeStruct((NX, 256, H...  9.85 us
    unnamed x20, local copies, waits for them, and re-layouts  6.8 us

profile of v1, /device:TPU:1, one launch (start us, length us, event | category | flops | bytes accessed | tf_op | source)
XLA Modules:
  0.0 105.6 jit_solution(10326255634210770968)
XLA Ops:
  0.0 0.0 copy-start.6
  0.0 0.0 copy-start.4
  0.0 0.0 copy-start.8
  0.0 0.0 copy-start.7
  0.0 1.9 %copy.10.blocks_ref = s32[64,32,16]{2,1,0:T(8,128)S(1)} copy(s32[64,32,16]{0,2,1:T(8,128)} %param.15) | data formatting | bytes 262144 | tf_op args[6]
  1.9 0.0 copy-start.1
  2.0 1.2 %copy-done.1 = bf16[512,1024]{1,0:T(8,128)(2,1)S(1)} copy-done((bf16[512,1024]{1,0:T(8,128)(2,1)S(1)}, bf16[512,1024]{1,0:T(8,128)(2,1)}, u32[]{:S(2)}) %copy-start.1) | copy-done | bytes 1048600
  3.2 0.0 copy-start.2
  3.2 1.2 %copy-done.2 = bf16[512,1024]{1,0:T(8,128)(2,1)S(1)} copy-done((bf16[512,1024]{1,0:T(8,128)(2,1)S(1)}, bf16[512,1024]{1,0:T(8,128)(2,1)}, u32[]{:S(2)}) %copy-start.2) | copy-done | bytes 1048600
  4.4 0.0 copy-start.3
  4.4 0.9 copy-done.3
  5.4 0.0 copy-start.5
  5.4 0.8 copy-done.5
  6.2 45.1 %spread.1 = (bf16[4,256,128]{2,1,0:T(8,128)(2,1)S(1)}, bf16[16,2,8,32,128]{4,3,2,1,0:T(8,128)(2,1)S(1)}, bf16[1024,1024]{1,0:T(8,128)(2,1)}) custom-call(bf16[4,8192]{1,0:T(4,128)(2,1)S(1)} %copy-done.5, bf16[512,1024]{1,0:T(8,128)(2,1)S(1)} %copy-done.1, bf16[512,1024]{1,0:T(8,128)(2,1)S(1)} %copy-done.2, bf16[256,512]{1,0:T(8,128)(2,1)S(1)} %copy-done.3), custom_call_target="tpu_custom_call" | custom-call | tf_op jit(solution)/shard_map/spread/pallas_call | solution.py:213
  51.3 0.0 copy-start
  51.3 0.0 copy-done.6
  51.3 0.0 copy-done.4
  51.3 0.0 copy-done.8
  51.4 0.0 copy-done.7
  51.4 9.9 %attend.1 = (bf16[4,256,128]{2,1,0:T(8,128)(2,1)S(1)}, f32[4,8,256]{2,1,0:T(8,128)S(1)}) custom-call(s32[64]{0:T(128)S(1)} %copy-done.7, s32[64]{0:T(128)S(1)} %copy-done.8, s32[64,32,16]{2,1,0:T(8,128)S(1)} %copy.10.blocks_ref, s32[64,1024]{1,0:T(8,128)S(1)} %copy-done.4, s32[64,128]{1,0:T(8,128)S(1)} %copy-done.6, ...), custom_call_target="tpu_custom_call" | custom-call | tf_op jit(solution)/shard_map/attend/pallas_call | solution.py:345
  61.2 0.0 copy-done
  61.2 43.7 %project.1 = bf16[4,8192]{1,0:T(4,128)(2,1)S(1)} custom-call(bf16[4,256,128]{2,1,0:T(8,128)(2,1)S(1)} %get-tuple-element.12.o_ref, f32[4,8,256]{2,1,0:T(8,128)S(1)} %get-tuple-element.13.st_ref, bf16[1024,1024]{1,0:T(8,128)(2,1)S(1)} %copy-done), custom_call_target="tpu_custom_call" | custom-call | tf_op jit(solution)/shard_map/project/pallas_call | solution.py:464
  105.0 0.6 copy.12
Async XLA Ops:
  0.0 51.3 %copy-start.6 = (s32[64,128]{1,0:T(8,128)S(1)}, s32[64,128]{1,0:T(8,128)}, u32[]{:S(2)}) copy-start(s32[64,128]{1,0:T(8,128)} %offs_ref.1) | copy-start | bytes 98308
  0.0 51.3 %copy-start.4 = (s32[64,1024]{1,0:T(8,128)S(1)}, s32[64,1024]{1,0:T(8,128)}, u32[]{:S(2)}) copy-start(s32[64,1024]{1,0:T(8,128)} %cols_ref.1) | copy-start | bytes 786436
  0.0 51.3 %copy-start.8 = (s32[64]{0:T(128)S(1)}, s32[64]{0:T(128)}, u32[]{:S(2)}) copy-start(s32[64]{0:T(128)} %count_ref.1) | copy-start | bytes 772
  0.0 51.4 %copy-start.7 = (s32[64]{0:T(128)S(1)}, s32[64]{0:T(128)}, u32[]{:S(2)}) copy-start(s32[64]{0:T(128)} %kind_ref.1) | copy-start | bytes 772
  1.9 1.2 %copy-start.1 = (bf16[512,1024]{1,0:T(8,128)(2,1)S(1)}, bf16[512,1024]{1,0:T(8,128)(2,1)}, u32[]{:S(2)}) copy-start(bf16[512,1024]{1,0:T(8,128)(2,1)} %k_ref.1) | copy-start | bytes 3145732
  3.2 1.2 %copy-start.2 = (bf16[512,1024]{1,0:T(8,128)(2,1)S(1)}, bf16[512,1024]{1,0:T(8,128)(2,1)}, u32[]{:S(2)}) copy-start(bf16[512,1024]{1,0:T(8,128)(2,1)} %v_ref.1) | copy-start | bytes 3145732
  4.4 0.9 copy-start.3
  5.4 0.8 copy-start.5
  51.3 9.9 %copy-start = (bf16[1024,1024]{1,0:T(8,128)(2,1)S(1)}, bf16[1024,1024]{1,0:T(8,128)(2,1)}, u32[]{:S(2)}) copy-start(bf16[1024,1024]{1,0:T(8,128)(2,1)} %get-tuple-element.14.w_ref) | copy-start | bytes 6291460

commit v2 on v0

v2 whole, which is shorter than its diff:
```python
import math

import jax
import jax.numpy as jnp
from jax import lax
from jax.experimental import pallas as pl
from jax.experimental.pallas import tpu as pltpu
from jax.sharding import PartitionSpec as P

H = 64
KVH = 8
HD = 128
NX, NZ, NY = 4, 8, 8
NT = 2 * NY
MASKED = -1e30
MESH = pl.DeviceIdType.MESH
F32 = jnp.float32
BF16 = jnp.bfloat16
SCALE = math.log2(math.e) / math.sqrt(HD)


def remote(src, dst, send_sem, recv_sem, ctx, tp):
    return pltpu.make_async_remote_copy(
        src_ref=src,
        dst_ref=dst,
        send_sem=send_sem,
        recv_sem=recv_sem,
        device_id=(ctx, tp),
        device_id_type=MESH,
    )


def arrived(ref, sem):
    pltpu.make_async_copy(ref, ref, sem).wait()


def lanes(shape):
    return lax.broadcasted_iota(jnp.int32, shape, len(shape) - 1)


def subs(shape):
    return lax.broadcasted_iota(jnp.int32, shape, 0)


def aligned(start, size):
    return pl.ds(pl.multiple_of(start, size), size)


def by_distance(i):
    odd = i % 2
    return odd * ((i + 1) // 2) + (1 - odd) * ((8 - i // 2) % 8)


def member_rows(values, rows, first_row):
    high = jnp.where(values // 128 == first_row, 1.0, 0.0).astype(BF16)
    low = jnp.where(values % 128 == subs((128, values.shape[1])), 1.0, 0.0).astype(BF16)
    found = lax.dot_general(high, low, (((1,), (1,)), ((), ())), preferred_element_type=F32)
    return jnp.where(found > 0.5, 0.0, MASKED)


def fill_masks(slash, count, head, x, y, blocks, cols8, offs8, row_bias, tile_bias):
    tile = subs((32, 1024))
    tile = 16 * (tile // 4) + 4 * x + tile % 4
    vertical = member_rows(cols8[pl.ds(y, 1), :], 32, tile)
    ids = jnp.where(lanes((32, 16, H)) == head, blocks[...].astype(F32), 0.0)
    ids = jnp.sum(ids, axis=2, keepdims=True)
    at = lanes((1, 1, 128))
    block = (8 * (4 * (at // 8) + x) + at % 8).astype(F32)
    turn = lax.broadcasted_iota(jnp.int32, (32, 16, 128), 1)
    hit = jnp.where(ids == block, 0.0, MASKED)
    hit = jnp.where(turn >= 1, jnp.where(turn < count, hit, MASKED), MASKED)
    chosen = jnp.max(hit, axis=1)
    left = lanes((32, 128)) < 64
    for i in range(32):
        pair = jnp.where(left, chosen[:, 2 * i : 2 * i + 1], chosen[:, 2 * i + 1 : 2 * i + 2])
        row_bias[i] = jnp.where(slash, jnp.broadcast_to(vertical[i : i + 1, :], (32, 128)), pair)
    rev = 511 - offs8[pl.ds(y, 1), :]
    phases = [member_rows(rev + 128 + 64 * phase, 8, subs((8, 128))) for phase in range(2)]
    back = subs((64, 128)) - lanes((64, 128))
    right = lanes((64, 128)) >= 64
    nothing = jnp.full((64, 128), MASKED, F32)
    tile_bias[0] = nothing
    tile_bias[11] = nothing
    for i in range(10):
        start = 576 - 64 * i
        phase = (start // 64) % 2
        first = (start + 64 * phase) // 128
        pair = jnp.concatenate(
            [phases[phase][first : first + 1, :], phases[phase][first + 1 : first + 2, :]], axis=1
        )
        rolled = pltpu.roll(jnp.broadcast_to(pair, (64, 256)), 256 - 63, 1, stride=1, stride_axis=0)
        own = nothing
        if i == 0:
            own = jnp.where(right, MASKED, jnp.where(back >= 0, 0.0, MASKED))
        if i == 1:
            own = jnp.where(right, jnp.where(back + 64 >= 0, 0.0, MASKED), MASKED)
        tile_bias[i + 1] = jnp.where(slash, rolled[:, :128], own)


def layer_kernel(
    q_ref, k_ref, v_ref, w_ref, kind_ref, count_ref, blocks_ref, cols_ref, offs_ref,
    out_ref,
    qv, qt, qs, q2, qf, qb, kvb, wv, blocks, cols8, offs8, row_bias, tile_bias,
    top, total, mixed, o_out, st_out, ob, sb, ab, part, rb, fb, fr,
    in_sem, q1_send, q1_recv, q2_send, q2_recv, qx_send, qx_recv,
    kz_send, kz_recv, ky_send, ky_recv, kc_send, kc_recv,
    w_send, w_recv, wc_send, wc_recv, ox_send, ox_recv,
    a_send, a_recv, z_send, z_recv, f_send, f_recv,
):
    ctx = lax.axis_index("ctx")
    t = lax.axis_index("tp")
    z, x, y, c = ctx // NX, ctx % NX, t // 2, t % 2
    zc = z // 4
    partner = 2 * y + 1 - c
    head = 8 * z + y

    loads = [
        pltpu.make_async_copy(q_ref, qv, in_sem.at[0]),
        pltpu.make_async_copy(blocks_ref, blocks, in_sem.at[1]),
        pltpu.make_async_copy(cols_ref.at[aligned(8 * z, 8)], cols8, in_sem.at[2]),
        pltpu.make_async_copy(offs_ref.at[aligned(8 * z, 8)], offs8, in_sem.at[3]),
    ]
    for copy in loads:
        copy.start()

    barrier = pltpu.get_barrier_semaphore()

    def greet(to_ctx, to_tp):
        pl.semaphore_signal(barrier, inc=1, device_id=(to_ctx, to_tp), device_id_type=MESH)

    for d in range(1, NT):
        greet(ctx, (t + d) % NT)
    for d in range(1, NZ):
        for cc in range(2):
            greet(((z + d) % NZ) * NX + x, 2 * y + cc)
    for d in range(1, NX):
        greet(z * NX + (x + d) % NX, t)

    loads[0].wait()
    for yy in range(NY):
        for g in range(KVH):
            at = (8 * g + yy) * HD
            qt[yy, g] = qv[:, at : at + HD]
    share = 2 * (y % 2) + c
    other = 2 * (1 - y % 2) + c

    def piece(zz, i, s):
        return kvb.at[zz, i, aligned(128 * s, 128)]

    rows = aligned(128 * share, 128)
    for i, ref in enumerate((k_ref, v_ref)):
        own = pltpu.make_async_copy(ref.at[rows, aligned(HD * z, HD)], piece(z, i, share), kz_recv.at[2 * z + i])
        own.start()
    w_own = pltpu.make_async_copy(w_ref, wv.at[aligned(256 * x, 256), aligned(512 * c, 512)], in_sem.at[4])
    w_own.start()

    pl.semaphore_wait(barrier, NT - 1 + 2 * (NZ - 1) + NX - 1)

    q1 = [
        remote(qt.at[(y + d) % NY], qs.at[t], q1_send.at[d], q1_recv, ctx, ((y + d) % NY) * 2 + zc)
        for d in range(NY)
    ]
    for d in range(1, NY):
        q1[d].start()

    @pl.when(zc == c)
    def _():
        pltpu.make_async_copy(qt.at[y], qs.at[t], q1_recv).start()

    @pl.when(zc != c)
    def _():
        q1[0].start()

    kz = []
    for d in (1, 7, 2, 6, 3, 5, 4):
        g = (z + d) % NZ
        for i, ref in enumerate((k_ref, v_ref)):
            copy = remote(
                ref.at[rows, aligned(HD * g, HD)], piece(z, i, share),
                kz_send.at[2 * d + i], kz_recv.at[2 * z + i], g * NX + x, t,
            )
            copy.start()
            kz.append(copy)

    def y_copy(zz, i):
        to = (y + 1) % NY if i == 0 else (y + NY - 1) % NY
        ref = piece(zz, i, share)
        return remote(ref, ref, ky_send.at[2 * zz + i], ky_recv.at[2 * zz + i], ctx, 2 * to + c)

    def core_copy(zz, i, s, n):
        ref = piece(zz, i, s)
        return remote(ref, ref, kc_send.at[4 * zz + 2 * n + i], kc_recv.at[zz], ctx, partner)

    def forward_own(i):
        zz = (z + by_distance(i)) % NZ
        for kv in range(2):
            arrived(piece(zz, kv, share), kz_recv.at[2 * zz + kv])
            y_copy(zz, kv).start()
            core_copy(zz, kv, share, 0).start()

    def forward_other(i):
        zz = (z + by_distance(i)) % NZ
        for kv in range(2):
            arrived(piece(zz, kv, other), ky_recv.at[2 * zz + kv])
            core_copy(zz, kv, other, 1).start()

    forward_own(0)

    def q2_copy(d):
        g = (z + d) % NZ
        return remote(qs.at[:, g], q2.at[z % 4], q2_send.at[d], q2_recv, g * NX + x, t)

    @pl.when(zc == c)
    def _():
        arrived(qs, q1_recv)
        for d in range(1, NZ):
            q2_copy(d).start()
        pltpu.make_async_copy(qs.at[:, z], q2.at[z % 4], q2_recv).start()

    for copy in loads[1:]:
        copy.wait()
    fill_masks(
        kind_ref[head] == 1, count_ref[head], head, x, y, blocks, cols8, offs8, row_bias, tile_bias
    )
    top[...] = jnp.full((NX, 256, 128), MASKED, F32)
    total[...] = jnp.zeros((NX, 256, 128), F32)
    mixed[...] = jnp.zeros((NX, 256, HD), F32)

    forward_own(1)

    arrived(q2, q2_recv)
    for i in range(64):
        qf[4 * i : 4 * i + 4, :] = q2[i // 16, i % 16].astype(F32)
    qb[x] = qf[...].astype(BF16)
    qx = [
        remote(qb.at[x], qb.at[x], qx_send.at[d], qx_recv.at[d], z * NX + (x + d) % NX, t)
        for d in range(1, NX)
    ]
    for copy in qx:
        copy.start()

    def w_view(xx, cc):
        return wv.at[aligned(256 * xx, 256), aligned(512 * cc, 512)]

    wx = [
        remote(w_ref, w_view(x, c), w_send.at[d], w_recv.at[d], z * NX + (x + d) % NX, t)
        for d in range(1, NX)
    ]
    for copy in wx:
        copy.start()
    wc = [remote(w_ref, w_view(x, c), wc_send.at[0], wc_recv, ctx, partner)]
    wc[0].start()

    forward_other(0)
    for d in range(1, NX):
        arrived(qb.at[(x + NX - d) % NX], qx_recv.at[d])

    def chunk(zz, band):
        keys = kvb[zz, 0]
        values = kvb[zz, 1]

        def group(xx, carry):
            s = lax.dot_general(qb[xx], keys, (((1,), (1,)), ((), ())), preferred_element_type=F32)
            weights = []
            factors = []
            for zl in range(4):
                b = 16 * c + 4 * zl + xx
                old = top[xx, 64 * zl : 64 * zl + 64]
                tiles = []
                high = None
                for w in range(4):
                    bias = row_bias[4 * zz + w, pl.ds(b, 1), :]
                    if band:
                        which = 225 + b - 8 * (4 * zz + x) - 2 * w
                        bias = jnp.maximum(bias, tile_bias[jnp.clip(which, 0, 11)])
                    tile = s[64 * zl : 64 * zl + 64, 128 * w : 128 * w + 128] * SCALE + bias
                    high = tile if high is None else jnp.maximum(high, tile)
                    tiles.append(tile)
                new = jnp.maximum(old, jnp.max(high, axis=1, keepdims=True))
                top[xx, 64 * zl : 64 * zl + 64] = new
                factor = jnp.exp2(old - new)
                tiles = [jnp.exp2(tile - new) for tile in tiles]
                total[xx, 64 * zl : 64 * zl + 64] = total[xx, 64 * zl : 64 * zl + 64] * factor + (
                    (tiles[0] + tiles[1]) + (tiles[2] + tiles[3])
                )
                factors.append(factor)
                weights.append(jnp.concatenate([tile.astype(BF16) for tile in tiles], axis=1))
            added = jnp.dot(jnp.concatenate(weights, axis=0), values, preferred_element_type=F32)
            mixed[xx] = mixed[xx] * jnp.concatenate(factors, axis=0) + added
            return carry

        lax.fori_loop(0, NX, group, 0)

    def step(i, carry):
        zz = (z + by_distance(i)) % NZ

        @pl.when(i < NZ - 2)
        def _():
            forward_own(i + 2)

        @pl.when(i < NZ - 1)
        def _():
            forward_other(i + 1)

        arrived(kvb.at[zz, 0], kc_recv.at[zz])

        @pl.when(zz >= 6)
        def _():
            chunk(zz, True)

        @pl.when(zz < 6)
        def _():
            chunk(zz, False)

        return carry

    lax.fori_loop(0, NZ, step, 0)

    ox = []
    for d in (2, 1, 3, 0):
        xx = (x + d) % NX
        amount = jnp.sum(total[xx], axis=1, keepdims=True)
        o_out[xx] = (mixed[xx] / amount).astype(BF16)
        st_out[xx] = (top[xx] + jnp.log2(amount)).T[:8, :]
        if d:
            for i, (src, dst) in enumerate(((st_out, sb), (o_out, ob))):
                copy = remote(
                    src.at[xx], dst.at[d], ox_send.at[2 * d + i], ox_recv.at[2 * d + i], z * NX + xx, t
                )
                copy.start()
                ox.append(copy)
    for d in range(1, NX):
        ref = w_view((x + NX - d) % NX, c)
        arrived(ref, w_recv.at[d])
        copy = remote(ref, ref, wc_send.at[d], wc_recv, ctx, partner)
        copy.start()
        wc.append(copy)
    for d in range(1, NX):
        arrived(sb.at[d], ox_recv.at[2 * d])
    levels = [st_out[x]] + [sb[d] for d in range(1, NX)]
    best = jnp.maximum(jnp.maximum(levels[0], levels[1]), jnp.maximum(levels[2], levels[3]))
    parts = [jnp.exp2(level - best) for level in levels]
    amount = (parts[0] + parts[1]) + (parts[2] + parts[3])
    parts = [p / amount for p in parts]
    table = jnp.concatenate(parts + [jnp.zeros((96, 256), F32)], axis=0).T
    for d in range(1, NX):
        arrived(ob.at[d], ox_recv.at[2 * d + 1])
    joined = table[:, 0:1] * o_out[x].astype(F32)
    for d in range(1, NX):
        joined = joined + table[:, 8 * d : 8 * d + 1] * ob[d].astype(F32)
    joined = joined.astype(BF16)
    for i in range(4):
        ab[i, :, aligned(HD * y, HD)] = joined[64 * i : 64 * i + 64, :]

    def a_copy(i, d):
        ref = ab.at[i, :, aligned(HD * y, HD)]
        return remote(ref, ref, a_send.at[8 * i + d], a_recv.at[i], ctx, 2 * ((y + d) % NY) + c)

    for j in range(4):
        for d in (4, 3, 5, 2, 6, 1, 7):
            a_copy((z + j) % 4, d).start()

    arrived(wv.at[:, pl.ds(0, 512)], wc_recv)
    w_own.wait()

    def z_copy(i, cc):
        return remote(
            part.at[i, cc], rb.at[z], z_send.at[2 * i + cc], z_recv, (4 * c + i) * NX + x, 2 * y + cc
        )

    for j in range(4):
        i = (z + j) % 4
        arrived(ab.at[i, :, pl.ds(0, 896)], a_recv.at[i])
        projected = jnp.dot(ab[i], wv[...], preferred_element_type=F32).astype(BF16)
        for cc in range(2):
            part[i, cc] = projected[:, 512 * cc : 512 * cc + 512]
            mine = jnp.logical_and(4 * c + i == z, cc == c)

            @pl.when(jnp.logical_not(mine))
            def _():
                z_copy(i, cc).start()

            @pl.when(mine)
            def _():
                pltpu.make_async_copy(part.at[i, cc], rb.at[z], z_recv).start()

    arrived(rb, z_recv)
    summed = rb[0].astype(F32)
    for g in range(1, NZ):
        summed = summed + rb[g].astype(F32)
    for tt in range(NT):
        fb[tt] = summed[4 * tt : 4 * tt + 4, :].astype(BF16)
    last = [
        remote(fb.at[(t + d) % NT], fr.at[t], f_send.at[d], f_recv, ctx, (t + d) % NT)
        for d in range(1, NT)
    ]
    for copy in last:
        copy.start()
    pltpu.make_async_copy(fb.at[t], fr.at[t], f_recv).start()

    for copy in q1[1:] + kz + qx + wx + wc + ox:
        copy.wait_send()

    @pl.when(zc != c)
    def _():
        q1[0].wait_send()

    @pl.when(zc == c)
    def _():
        for d in range(1, NZ):
            q2_copy(d).wait_send()

    def sent(zz, carry):
        for kv in range(2):
            y_copy(zz, kv).wait_send()
            core_copy(zz, kv, share, 0).wait_send()
            core_copy(zz, kv, other, 1).wait_send()
        return carry

    lax.fori_loop(0, NZ, sent, 0)
    for i in range(4):
        for d in range(1, NY):
            a_copy(i, d).wait_send()
        for cc in range(2):
            mine = jnp.logical_and(4 * c + i == z, cc == c)

            @pl.when(jnp.logical_not(mine))
            def _():
                z_copy(i, cc).wait_send()

    arrived(fr, f_recv)
    for tt in range(NT):
        out_ref[:, 512 * tt : 512 * tt + 512] = fr[tt]
    for copy in last:
        copy.wait_send()


def layer(q, k, v, w, kinds, counts, blocks, cols, offs):
    dma = pltpu.SemaphoreType.DMA
    hbm = pl.BlockSpec(memory_space=pltpu.HBM)
    smem = pl.BlockSpec(memory_space=pltpu.SMEM)
    vmem = pltpu.VMEM
    return pl.pallas_call(
        layer_kernel,
        out_shape=jax.ShapeDtypeStruct((4, 8192), BF16),
        in_specs=[hbm, hbm, hbm, hbm, smem, smem, hbm, hbm, hbm],
        out_specs=pl.BlockSpec(memory_space=pltpu.VMEM),
        scratch_shapes=[
            vmem((4, 8192), BF16),
            vmem((NY, KVH, 4, HD), BF16),
            vmem((NT, KVH, 4, HD), BF16),
            vmem((4, NT, 4, HD), BF16),
            vmem((256, HD), F32),
            vmem((NX, 256, HD), BF16),
            vmem((NZ, 2, 512, HD), BF16),
            vmem((1024, 1024), BF16),
            vmem((32, 16, H), jnp.int32),
            vmem((8, 1024), jnp.int32),
            vmem((8, 128), jnp.int32),
            vmem((32, 32, 128), F32),
            vmem((12, 64, 128), F32),
            vmem((NX, 256, 128), F32),
            vmem((NX, 256, 128), F32),
            vmem((NX, 256, HD), F32),
            vmem((NX, 256, HD), BF16),
            vmem((NX, 8, 256), F32),
            vmem((NX, 256, HD), BF16),
            vmem((NX, 8, 256), F32),
            vmem((4, 64, 1024), BF16),
            vmem((4, 2, 64, 512), BF16),
            vmem((NZ, 64, 512), BF16),
            vmem((NT, 4, 512), BF16),
            vmem((NT, 4, 512), BF16),
            dma((5,)),
            dma((8,)), dma, dma((8,)), dma, dma((4,)), dma((4,)),
            dma((16,)), dma((16,)), dma((16,)), dma((16,)), dma((32,)), dma((8,)),
            dma((4,)), dma((4,)), dma((4,)), dma, dma((8,)), dma((8,)),
            dma((32,)), dma((4,)), dma((8,)), dma, dma((16,)), dma,
        ],
        compiler_params=pltpu.CompilerParams(
            collective_id=0, has_side_effects=True, vmem_limit_bytes=56 * 1024 * 1024
        ),
        name="layer",
    )(q, k, v, w, kinds, counts, blocks, cols, offs)


def shards(q, k, v, w, kinds, counts, blocks, cols, offs):
    return layer(q, k, v, w, kinds, counts, blocks.transpose(1, 2, 0), cols, offs)


def solution(mesh):
    return jax.shard_map(
        shards,
        mesh=mesh,
        in_specs=(
            P(("ctx", "tp"), None),
            P("ctx", None),
            P("ctx", None),
            P("ctx", "tp"),
            P(),
            P(),
            P(),
            P(),
            P(),
        ),
        out_specs=P(("ctx", "tp"), None),
        check_vma=False,
    )
```

time: 920 us -> 94.5 us (0.10)
  local copies, waits for them, and re-layouts: 443 us -> 1.49 us
  waiting for transfers between devices: 385 us -> 0 us
  Pallas kernels: 0 us -> 92.8 us
  starting transfers between devices: 28.6 us -> 0 us
  matrix products: 24.2 us -> 0 us
  other arithmetic: 16.4 us -> 0 us
  between operations: 15.5 us -> 0.01 us
    gather x206 -> x0, local copies, waits for them, and re-layouts: 428 us -> none
    unnamed x3 -> x0, waiting for transfers between devices: 206 us -> none
    all_to_all x3 -> x0, waiting for transfers between devices: 179 us -> none  [the longest x1 87.8 us: shards(): lax.all_to_all(local_keys[:, kv_target, :], 'ctx', split_axis=1, concat_a...]
    pallas_call x0 -> x1, Pallas kernels: none -> 92.8 us  [layer(): pl.pallas_call(layer_kernel, out_shape=jax.ShapeDtypeStruct((4, 8192), BF...]
    all_to_all x3 -> x0, starting transfers between devices: 28.5 us -> none  [the longest x1 13.8 us: shards(): lax.all_to_all(q_slab, 'ctx', split_axis=1, concat_axis=0, tiled=True)]
    dot_general x9 -> x0, matrix products: 24.2 us -> none  [the longest x2 6.89 us: score_turn(): jnp.einsum('gqd,gkd->gqk', query_groups, key_rows, preferred_element_type...]
    reduce_or x1 -> x0, other arithmetic: 10.7 us -> none  [slash_pattern(): jnp.any(distance[:, :, None] == offsets[None, None, :], axis=2)]
  transfers between devices with their start and end apart: 5 -> 0, of which waited for: 4 -> 0; matrix products, arithmetic and copies ran while one was open for 52% -> 0% of each run, Pallas kernels for 0% -> 0%
where the time goes in v2:
time: 94.5 us; the launch traced here: 94.3 us
  Pallas kernels  92.8 us (98%)
  local copies, waits for them, and re-layouts  1.49 us (2%)
    pallas_call x1, Pallas kernels, layer(): pl.pallas_call(layer_kernel, out_shape=jax.ShapeDtypeStruct((4, 8192), BF...  92.8 us

profile of v2, /device:TPU:1, one launch (start us, length us, event | category | flops | bytes accessed | tf_op | source)
XLA Modules:
  0.0 94.3 jit_solution(1160724786583459479)
XLA Ops:
  0.0 92.8 %layer.1 = bf16[4,8192]{1,0:T(4,128)(2,1)} custom-call(bf16[4,8192]{1,0:T(4,128)(2,1)} %q_ref.1, bf16[512,1024]{1,0:T(8,128)(2,1)} %k_ref.1, bf16[512,1024]{1,0:T(8,128)(2,1)} %v_ref.1, bf16[256,512]{1,0:T(8,128)(2,1)} %w_ref.1, s32[64]{0:T(128)} %kind_ref.1, s32[64]{0:T(128)} %count_ref.1, s32[32,16,64]{2,1,0:T(8,128)} %bitcast.1, s32[64,1024]{1,0:T(8,128)} %cols_ref.1, ...), custom_call_target="tpu_custom_call" | custom-call | tf_op jit(solution)/shard_map/layer/pallas_call | solution.py:443
  92.8 1.5 %copy.11 = bf16[4,8192]{1,0:T(4,128)(2,1)} copy(bf16[4,8192]{1,0:T(4,128)(2,1)} %layer.1) | data formatting | bytes 131072

commit v3 on v2

--- a/solution.py
+++ b/solution.py
@@ -51,7 +51,7 @@
     return odd * ((i + 1) // 2) + (1 - odd) * ((8 - i // 2) % 8)
 
 
-def member_rows(values, rows, first_row):
+def member_rows(values, first_row):
     high = jnp.where(values // 128 == first_row, 1.0, 0.0).astype(BF16)
     low = jnp.where(values % 128 == subs((128, values.shape[1])), 1.0, 0.0).astype(BF16)
     found = lax.dot_general(high, low, (((1,), (1,)), ((), ())), preferred_element_type=F32)
@@ -61,7 +61,7 @@
 def fill_masks(slash, count, head, x, y, blocks, cols8, offs8, row_bias, tile_bias):
     tile = subs((32, 1024))
     tile = 16 * (tile // 4) + 4 * x + tile % 4
-    vertical = member_rows(cols8[pl.ds(y, 1), :], 32, tile)
+    vertical = member_rows(cols8[pl.ds(y, 1), :], tile)
     ids = jnp.where(lanes((32, 16, H)) == head, blocks[...].astype(F32), 0.0)
     ids = jnp.sum(ids, axis=2, keepdims=True)
     at = lanes((1, 1, 128))
@@ -75,7 +75,7 @@
         pair = jnp.where(left, chosen[:, 2 * i : 2 * i + 1], chosen[:, 2 * i + 1 : 2 * i + 2])
         row_bias[i] = jnp.where(slash, jnp.broadcast_to(vertical[i : i + 1, :], (32, 128)), pair)
     rev = 511 - offs8[pl.ds(y, 1), :]
-    phases = [member_rows(rev + 128 + 64 * phase, 8, subs((8, 128))) for phase in range(2)]
+    phases = [member_rows(rev + 128 + 64 * phase, subs((8, 128))) for phase in range(2)]
     back = subs((64, 128)) - lanes((64, 128))
     right = lanes((64, 128)) >= 64
     nothing = jnp.full((64, 128), MASKED, F32)
@@ -100,7 +100,7 @@
 def layer_kernel(
     q_ref, k_ref, v_ref, w_ref, kind_ref, count_ref, blocks_ref, cols_ref, offs_ref,
     out_ref,
-    qv, qt, qs, q2, qf, qb, kvb, wv, blocks, cols8, offs8, row_bias, tile_bias,
+    qv, qt, qs, qy, q4, qf, qb, kl, kvb, wv, blocks, cols8, offs8, row_bias, tile_bias,
     top, total, mixed, o_out, st_out, ob, sb, ab, part, rb, fb, fr,
     in_sem, q1_send, q1_recv, q2_send, q2_recv, qx_send, qx_recv,
     kz_send, kz_recv, ky_send, ky_recv, kc_send, kc_recv,
@@ -110,7 +110,6 @@
     ctx = lax.axis_index("ctx")
     t = lax.axis_index("tp")
     z, x, y, c = ctx // NX, ctx % NX, t // 2, t % 2
-    zc = z // 4
     partner = 2 * y + 1 - c
     head = 8 * z + y
 
@@ -140,7 +139,7 @@
     for yy in range(NY):
         for g in range(KVH):
             at = (8 * g + yy) * HD
-            qt[yy, g] = qv[:, at : at + HD]
+            qt[g, yy] = qv[:, at : at + HD]
     share = 2 * (y % 2) + c
     other = 2 * (1 - y % 2) + c
 
@@ -148,35 +147,36 @@
         return kvb.at[zz, i, aligned(128 * s, 128)]
 
     rows = aligned(128 * share, 128)
+    dense = []
     for i, ref in enumerate((k_ref, v_ref)):
-        own = pltpu.make_async_copy(ref.at[rows, aligned(HD * z, HD)], piece(z, i, share), kz_recv.at[2 * z + i])
-        own.start()
-    w_own = pltpu.make_async_copy(w_ref, wv.at[aligned(256 * x, 256), aligned(512 * c, 512)], in_sem.at[4])
+        pltpu.make_async_copy(
+            ref.at[rows, aligned(HD * z, HD)], piece(z, i, share), kz_recv.at[2 * z + i]
+        ).start()
+        for d in range(1, NZ):
+            cols = aligned(HD * ((z + d) % NZ), HD)
+            dense.append(pltpu.make_async_copy(ref.at[rows, cols], kl.at[i, d], in_sem.at[5 + 8 * i + d]))
+            dense[-1].start()
+    w_own = pltpu.make_async_copy(w_ref, wv.at[c, x], in_sem.at[4])
     w_own.start()
 
+    for copy in dense:
+        copy.wait()
     pl.semaphore_wait(barrier, NT - 1 + 2 * (NZ - 1) + NX - 1)
 
     q1 = [
-        remote(qt.at[(y + d) % NY], qs.at[t], q1_send.at[d], q1_recv, ctx, ((y + d) % NY) * 2 + zc)
-        for d in range(NY)
+        remote(qt.at[(z + d) % NZ], qs.at[z], q1_send.at[d], q1_recv, ((z + d) % NZ) * NX + x, t)
+        for d in range(1, NZ)
     ]
-    for d in range(1, NY):
-        q1[d].start()
-
-    @pl.when(zc == c)
-    def _():
-        pltpu.make_async_copy(qt.at[y], qs.at[t], q1_recv).start()
-
-    @pl.when(zc != c)
-    def _():
-        q1[0].start()
+    for copy in q1:
+        copy.start()
+    pltpu.make_async_copy(qt.at[z], qs.at[z], q1_recv).start()
 
     kz = []
     for d in (1, 7, 2, 6, 3, 5, 4):
         g = (z + d) % NZ
-        for i, ref in enumerate((k_ref, v_ref)):
+        for i in range(2):
             copy = remote(
-                ref.at[rows, aligned(HD * g, HD)], piece(z, i, share),
+                kl.at[i, d], piece(z, i, share),
                 kz_send.at[2 * d + i], kz_recv.at[2 * z + i], g * NX + x, t,
             )
             copy.start()
@@ -205,17 +205,6 @@
             core_copy(zz, kv, other, 1).start()
 
     forward_own(0)
-
-    def q2_copy(d):
-        g = (z + d) % NZ
-        return remote(qs.at[:, g], q2.at[z % 4], q2_send.at[d], q2_recv, g * NX + x, t)
-
-    @pl.when(zc == c)
-    def _():
-        arrived(qs, q1_recv)
-        for d in range(1, NZ):
-            q2_copy(d).start()
-        pltpu.make_async_copy(qs.at[:, z], q2.at[z % 4], q2_recv).start()
 
     for copy in loads[1:]:
         copy.wait()
@@ -226,11 +215,26 @@
     total[...] = jnp.zeros((NX, 256, 128), F32)
     mixed[...] = jnp.zeros((NX, 256, HD), F32)
 
+    arrived(qs, q1_recv)
+    for yy in range(NY):
+        for zz in range(NZ):
+            qy[yy, zz] = qs[zz, yy]
+    q2 = []
+    for d in range(1, NT):
+        tt = (t + d) % NT
+        src = qy.at[tt // 2, pl.ds(4 * (tt % 2), 4)]
+        q2.append(remote(src, q4.at[t], q2_send.at[d], q2_recv, ctx, tt))
+        q2[-1].start()
+    pltpu.make_async_copy(qy.at[y, pl.ds(4 * c, 4)], q4.at[t], q2_recv).start()
+
     forward_own(1)
-
-    arrived(q2, q2_recv)
-    for i in range(64):
-        qf[4 * i : 4 * i + 4, :] = q2[i // 16, i % 16].astype(F32)
+    forward_own(2)
+    forward_other(0)
+
+    arrived(q4, q2_recv)
+    for zl in range(4):
+        for tt in range(NT):
+            qf[zl, 4 * tt : 4 * tt + 4, :] = q4[tt, zl].astype(F32)
     qb[x] = qf[...].astype(BF16)
     qx = [
         remote(qb.at[x], qb.at[x], qx_send.at[d], qx_recv.at[d], z * NX + (x + d) % NX, t)
@@ -239,68 +243,64 @@
     for copy in qx:
         copy.start()
 
-    def w_view(xx, cc):
-        return wv.at[aligned(256 * xx, 256), aligned(512 * cc, 512)]
-
     wx = [
-        remote(w_ref, w_view(x, c), w_send.at[d], w_recv.at[d], z * NX + (x + d) % NX, t)
+        remote(w_ref, wv.at[c, x], w_send.at[d], w_recv.at[d], z * NX + (x + d) % NX, t)
         for d in range(1, NX)
     ]
     for copy in wx:
         copy.start()
-    wc = [remote(w_ref, w_view(x, c), wc_send.at[0], wc_recv, ctx, partner)]
+    wc = [remote(w_ref, wv.at[c, x], wc_send.at[0], wc_recv, ctx, partner)]
     wc[0].start()
 
-    forward_other(0)
+    for i in range(3, 7):
+        forward_own(i)
+        forward_other(i - 2)
     for d in range(1, NX):
         arrived(qb.at[(x + NX - d) % NX], qx_recv.at[d])
+    forward_own(7)
 
     def chunk(zz, band):
         keys = kvb[zz, 0]
         values = kvb[zz, 1]
 
-        def group(xx, carry):
-            s = lax.dot_general(qb[xx], keys, (((1,), (1,)), ((), ())), preferred_element_type=F32)
-            weights = []
-            factors = []
-            for zl in range(4):
-                b = 16 * c + 4 * zl + xx
-                old = top[xx, 64 * zl : 64 * zl + 64]
-                tiles = []
-                high = None
-                for w in range(4):
-                    bias = row_bias[4 * zz + w, pl.ds(b, 1), :]
-                    if band:
-                        which = 225 + b - 8 * (4 * zz + x) - 2 * w
-                        bias = jnp.maximum(bias, tile_bias[jnp.clip(which, 0, 11)])
-                    tile = s[64 * zl : 64 * zl + 64, 128 * w : 128 * w + 128] * SCALE + bias
-                    high = tile if high is None else jnp.maximum(high, tile)
-                    tiles.append(tile)
-                new = jnp.maximum(old, jnp.max(high, axis=1, keepdims=True))
-                top[xx, 64 * zl : 64 * zl + 64] = new
-                factor = jnp.exp2(old - new)
-                tiles = [jnp.exp2(tile - new) for tile in tiles]
-                total[xx, 64 * zl : 64 * zl + 64] = total[xx, 64 * zl : 64 * zl + 64] * factor + (
-                    (tiles[0] + tiles[1]) + (tiles[2] + tiles[3])
-                )
-                factors.append(factor)
-                weights.append(jnp.concatenate([tile.astype(BF16) for tile in tiles], axis=1))
-            added = jnp.dot(jnp.concatenate(weights, axis=0), values, preferred_element_type=F32)
-            mixed[xx] = mixed[xx] * jnp.concatenate(factors, axis=0) + added
-            return carry
-
-        lax.fori_loop(0, NX, group, 0)
+        queries = qb[...].reshape(1024, HD)
+        s = lax.dot_general(queries, keys, (((1,), (1,)), ((), ())), preferred_element_type=F32)
+        weights = []
+        factors = []
+        for n in range(16):
+            xx, zl = n // 4, n % 4
+            b = 16 * c + 4 * zl + xx
+            old = top[xx, 64 * zl : 64 * zl + 64]
+            tiles = []
+            high = None
+            for w in range(4):
+                bias = row_bias[4 * zz + w, pl.ds(b, 1), :]
+                if band:
+                    which = 225 + b - 8 * (4 * zz + x) - 2 * w
+                    bias = jnp.maximum(bias, tile_bias[jnp.clip(which, 0, 11)])
+                tile = s[64 * n : 64 * n + 64, 128 * w : 128 * w + 128] * SCALE + bias
+                high = tile if high is None else jnp.maximum(high, tile)
+                tiles.append(tile)
+            new = jnp.maximum(old, jnp.max(high, axis=1, keepdims=True))
+            top[xx, 64 * zl : 64 * zl + 64] = new
+            factor = jnp.exp2(old - new)
+            tiles = [jnp.exp2(tile - new) for tile in tiles]
+            total[xx, 64 * zl : 64 * zl + 64] = total[xx, 64 * zl : 64 * zl + 64] * factor + (
+                (tiles[0] + tiles[1]) + (tiles[2] + tiles[3])
+            )
+            factors.append(factor)
+            weights.append(jnp.concatenate([tile.astype(BF16) for tile in tiles], axis=1))
+        added = jnp.dot(jnp.concatenate(weights, axis=0), values, preferred_element_type=F32)
+        for n in range(16):
+            at = (n // 4, pl.ds(64 * (n % 4), 64))
+            mixed[at] = mixed[at] * factors[n] + added[64 * n : 64 * n + 64]
 
     def step(i, carry):
         zz = (z + by_distance(i)) % NZ
 
-        @pl.when(i < NZ - 2)
+        @pl.when(i < NZ - 5)
         def _():
-            forward_own(i + 2)
-
-        @pl.when(i < NZ - 1)
-        def _():
-            forward_other(i + 1)
+            forward_other(i + 5)
 
         arrived(kvb.at[zz, 0], kc_recv.at[zz])
 
@@ -330,7 +330,7 @@
                 copy.start()
                 ox.append(copy)
     for d in range(1, NX):
-        ref = w_view((x + NX - d) % NX, c)
+        ref = wv.at[c, (x + NX - d) % NX]
         arrived(ref, w_recv.at[d])
         copy = remote(ref, ref, wc_send.at[d], wc_recv, ctx, partner)
         copy.start()
@@ -350,17 +350,17 @@
         joined = joined + table[:, 8 * d : 8 * d + 1] * ob[d].astype(F32)
     joined = joined.astype(BF16)
     for i in range(4):
-        ab[i, :, aligned(HD * y, HD)] = joined[64 * i : 64 * i + 64, :]
+        ab[i, y] = joined[64 * i : 64 * i + 64, :]
 
     def a_copy(i, d):
-        ref = ab.at[i, :, aligned(HD * y, HD)]
+        ref = ab.at[i, y]
         return remote(ref, ref, a_send.at[8 * i + d], a_recv.at[i], ctx, 2 * ((y + d) % NY) + c)
 
     for j in range(4):
         for d in (4, 3, 5, 2, 6, 1, 7):
             a_copy((z + j) % 4, d).start()
 
-    arrived(wv.at[:, pl.ds(0, 512)], wc_recv)
+    arrived(wv.at[0], wc_recv)
     w_own.wait()
 
     def z_copy(i, cc):
@@ -370,10 +370,11 @@
 
     for j in range(4):
         i = (z + j) % 4
-        arrived(ab.at[i, :, pl.ds(0, 896)], a_recv.at[i])
-        projected = jnp.dot(ab[i], wv[...], preferred_element_type=F32).astype(BF16)
+        arrived(ab.at[i, pl.ds(0, NY - 1)], a_recv.at[i])
+        features = jnp.concatenate([ab[i, yy] for yy in range(NY)], axis=1)
         for cc in range(2):
-            part[i, cc] = projected[:, 512 * cc : 512 * cc + 512]
+            weight = wv[cc].reshape(1024, 512)
+            part[i, cc] = jnp.dot(features, weight, preferred_element_type=F32).astype(BF16)
             mine = jnp.logical_and(4 * c + i == z, cc == c)
 
             @pl.when(jnp.logical_not(mine))
@@ -398,17 +399,8 @@
         copy.start()
     pltpu.make_async_copy(fb.at[t], fr.at[t], f_recv).start()
 
-    for copy in q1[1:] + kz + qx + wx + wc + ox:
+    for copy in q1 + q2 + kz + qx + wx + wc + ox:
         copy.wait_send()
-
-    @pl.when(zc != c)
-    def _():
-        q1[0].wait_send()
-
-    @pl.when(zc == c)
-    def _():
-        for d in range(1, NZ):
-            q2_copy(d).wait_send()
 
     def sent(zz, carry):
         for kv in range(2):
@@ -447,13 +439,15 @@
         out_specs=pl.BlockSpec(memory_space=pltpu.VMEM),
         scratch_shapes=[
             vmem((4, 8192), BF16),
-            vmem((NY, KVH, 4, HD), BF16),
-            vmem((NT, KVH, 4, HD), BF16),
-            vmem((4, NT, 4, HD), BF16),
-            vmem((256, HD), F32),
-            vmem((NX, 256, HD), BF16),
+            vmem((KVH, NY, 4, HD), BF16),
+            vmem((NZ, NY, 4, HD), BF16),
+            vmem((NY, NZ, 4, HD), BF16),
+            vmem((NT, 4, 4, HD), BF16),
+            vmem((4, 64, HD), F32),
+            vmem((NX, 4, 64, HD), BF16),
+            vmem((2, NZ, 128, HD), BF16),
             vmem((NZ, 2, 512, HD), BF16),
-            vmem((1024, 1024), BF16),
+            vmem((2, NX, 256, 512), BF16),
             vmem((32, 16, H), jnp.int32),
             vmem((8, 1024), jnp.int32),
             vmem((8, 128), jnp.int32),
@@ -466,13 +460,13 @@
             vmem((NX, 8, 256), F32),
             vmem((NX, 256, HD), BF16),
             vmem((NX, 8, 256), F32),
-            vmem((4, 64, 1024), BF16),
+            vmem((4, NY, 64, HD), BF16),
             vmem((4, 2, 64, 512), BF16),
             vmem((NZ, 64, 512), BF16),
             vmem((NT, 4, 512), BF16),
             vmem((NT, 4, 512), BF16),
-            dma((5,)),
-            dma((8,)), dma, dma((8,)), dma, dma((4,)), dma((4,)),
+            dma((21,)),
+            dma((8,)), dma, dma((16,)), dma, dma((4,)), dma((4,)),
             dma((16,)), dma((16,)), dma((16,)), dma((16,)), dma((32,)), dma((8,)),
             dma((4,)), dma((4,)), dma((4,)), dma, dma((8,)), dma((8,)),
             dma((32,)), dma((4,)), dma((8,)), dma, dma((16,)), dma,

time: 94.5 us -> 77.5 us (0.82)
  Pallas kernels: 92.8 us -> 75.8 us
    pallas_call x1, Pallas kernels: 92.8 us -> 75.8 us  [layer(): pl.pallas_call(layer_kernel, out_shape=jax.ShapeDtypeStruct((4, 8192), BF...]
where the time goes in v3:
time: 77.5 us; the launch traced here: 77.3 us
  Pallas kernels  75.8 us (98%)
  local copies, waits for them, and re-layouts  1.49 us (2%)
    pallas_call x1, Pallas kernels, layer(): pl.pallas_call(layer_kernel, out_shape=jax.ShapeDtypeStruct((4, 8192), BF...  75.8 us

profile of v3, /device:TPU:1, one launch (start us, length us, event | category | flops | bytes accessed | tf_op | source)
XLA Modules:
  0.0 77.3 jit_solution(13514261481694142790)
XLA Ops:
  0.0 75.8 %layer.1 = bf16[4,8192]{1,0:T(4,128)(2,1)} custom-call(bf16[4,8192]{1,0:T(4,128)(2,1)} %q_ref.1, bf16[512,1024]{1,0:T(8,128)(2,1)} %k_ref.1, bf16[512,1024]{1,0:T(8,128)(2,1)} %v_ref.1, bf16[256,512]{1,0:T(8,128)(2,1)} %w_ref.1, s32[64]{0:T(128)} %kind_ref.1, s32[64]{0:T(128)} %count_ref.1, s32[32,16,64]{2,1,0:T(8,128)} %bitcast.1, s32[64,1024]{1,0:T(8,128)} %cols_ref.1, ...), custom_call_target="tpu_custom_call" | custom-call | tf_op jit(solution)/shard_map/layer/pallas_call | solution.py:435
  75.8 1.5 %copy.11 = bf16[4,8192]{1,0:T(4,128)(2,1)} copy(bf16[4,8192]{1,0:T(4,128)(2,1)} %layer.1) | data formatting | bytes 131072

commit v4 on v3

--- a/solution.py
+++ b/solution.py
@@ -182,6 +182,15 @@
             copy.start()
             kz.append(copy)
 
+    wx = [
+        remote(w_ref, wv.at[c, x], w_send.at[d], w_recv.at[d], z * NX + (x + d) % NX, t)
+        for d in range(1, NX)
+    ]
+    for copy in wx:
+        copy.start()
+    wc = [remote(w_ref, wv.at[c, x], wc_send.at[0], wc_recv, ctx, partner)]
+    wc[0].start()
+
     def y_copy(zz, i):
         to = (y + 1) % NY if i == 0 else (y + NY - 1) % NY
         ref = piece(zz, i, share)
@@ -242,15 +251,6 @@
     ]
     for copy in qx:
         copy.start()
-
-    wx = [
-        remote(w_ref, wv.at[c, x], w_send.at[d], w_recv.at[d], z * NX + (x + d) % NX, t)
-        for d in range(1, NX)
-    ]
-    for copy in wx:
-        copy.start()
-    wc = [remote(w_ref, wv.at[c, x], wc_send.at[0], wc_recv, ctx, partner)]
-    wc[0].start()
 
     for i in range(3, 7):
         forward_own(i)
@@ -330,12 +330,6 @@
                 copy.start()
                 ox.append(copy)
     for d in range(1, NX):
-        ref = wv.at[c, (x + NX - d) % NX]
-        arrived(ref, w_recv.at[d])
-        copy = remote(ref, ref, wc_send.at[d], wc_recv, ctx, partner)
-        copy.start()
-        wc.append(copy)
-    for d in range(1, NX):
         arrived(sb.at[d], ox_recv.at[2 * d])
     levels = [st_out[x]] + [sb[d] for d in range(1, NX)]
     best = jnp.maximum(jnp.maximum(levels[0], levels[1]), jnp.maximum(levels[2], levels[3]))
@@ -360,6 +354,12 @@
         for d in (4, 3, 5, 2, 6, 1, 7):
             a_copy((z + j) % 4, d).start()
 
+    for d in range(1, NX):
+        ref = wv.at[c, (x + NX - d) % NX]
+        arrived(ref, w_recv.at[d])
+        copy = remote(ref, ref, wc_send.at[d], wc_recv, ctx, partner)
+        copy.start()
+        wc.append(copy)
     arrived(wv.at[0], wc_recv)
     w_own.wait()
 

time: 77.5 us -> 76.2 us (0.983); the launches traced: 77.3 us -> 75.1 us
  Pallas kernels: 75.8 us -> 73.6 us
    pallas_call x1, Pallas kernels: 75.8 us -> 73.6 us  [layer(): pl.pallas_call(layer_kernel, out_shape=jax.ShapeDtypeStruct((4, 8192), BF...]
where the time goes in v4:
time: 76.2 us; the launch traced here: 75.1 us
  Pallas kernels  73.6 us (97%)
  local copies, waits for them, and re-layouts  1.49 us (2%)
    pallas_call x1, Pallas kernels, layer(): pl.pallas_call(layer_kernel, out_shape=jax.ShapeDtypeStruct((4, 8192), BF...  73.6 us

profile of v4, /device:TPU:1, one launch (start us, length us, event | category | flops | bytes accessed | tf_op | source)
XLA Modules:
  0.0 75.1 jit_solution(9603189808316849898)
XLA Ops:
  0.0 73.6 %layer.1 = bf16[4,8192]{1,0:T(4,128)(2,1)} custom-call(bf16[4,8192]{1,0:T(4,128)(2,1)} %q_ref.1, bf16[512,1024]{1,0:T(8,128)(2,1)} %k_ref.1, bf16[512,1024]{1,0:T(8,128)(2,1)} %v_ref.1, bf16[256,512]{1,0:T(8,128)(2,1)} %w_ref.1, s32[64]{0:T(128)} %kind_ref.1, s32[64]{0:T(128)} %count_ref.1, s32[32,16,64]{2,1,0:T(8,128)} %bitcast.1, s32[64,1024]{1,0:T(8,128)} %cols_ref.1, ...), custom_call_target="tpu_custom_call" | custom-call | tf_op jit(solution)/shard_map/layer/pallas_call | solution.py:435
  73.6 1.5 %copy.11 = bf16[4,8192]{1,0:T(4,128)(2,1)} copy(bf16[4,8192]{1,0:T(4,128)(2,1)} %layer.1) | data formatting | bytes 131072

commit v5 on v3

--- a/solution.py
+++ b/solution.py
@@ -101,10 +101,10 @@
     q_ref, k_ref, v_ref, w_ref, kind_ref, count_ref, blocks_ref, cols_ref, offs_ref,
     out_ref,
     qv, qt, qs, qy, q4, qf, qb, kl, kvb, wv, blocks, cols8, offs8, row_bias, tile_bias,
-    top, total, mixed, o_out, st_out, ob, sb, ab, part, rb, fb, fr,
+    top, total, mixed, o_out, st_out, ob, sb, share_of, ab, part, rb, fb, fr,
     in_sem, q1_send, q1_recv, q2_send, q2_recv, qx_send, qx_recv,
     kz_send, kz_recv, ky_send, ky_recv, kc_send, kc_recv,
-    w_send, w_recv, wc_send, wc_recv, ox_send, ox_recv,
+    w_send, w_recv, wc_send, wc_recv, st_send, st_recv, ox_send, ox_recv,
     a_send, a_recv, z_send, z_recv, f_send, f_recv,
 ):
     ctx = lax.axis_index("ctx")
@@ -245,12 +245,19 @@
 
     wx = [
         remote(w_ref, wv.at[c, x], w_send.at[d], w_recv.at[d], z * NX + (x + d) % NX, t)
-        for d in range(1, NX)
+        for d in (1, 3)
     ]
-    for copy in wx:
+    wc = [remote(w_ref, wv.at[c, x], wc_send.at[0], wc_recv, ctx, partner)]
+    for copy in wx + wc:
         copy.start()
-    wc = [remote(w_ref, wv.at[c, x], wc_send.at[0], wc_recv, ctx, partner)]
-    wc[0].start()
+
+    def w_relay(d):
+        ref = wv.at[c, (x + NX - d) % NX, pl.ds(64 * (d - 1), 128)]
+        return remote(ref, ref, w_send.at[d - 1], w_recv.at[d - 1], z * NX + (x + d) % NX, t)
+
+    def w_core(d):
+        ref = wv.at[c, (x + NX - d) % NX]
+        return remote(ref, ref, wc_send.at[d], wc_recv, ctx, partner)
 
     for i in range(3, 7):
         forward_own(i)
@@ -302,6 +309,13 @@
         def _():
             forward_other(i + 5)
 
+        @pl.when(i == 5)
+        def _():
+            for d in (1, 3):
+                arrived(wv.at[c, (x + NX - d) % NX], w_recv.at[d])
+                w_relay(d).start()
+                w_core(d).start()
+
         arrived(kvb.at[zz, 0], kc_recv.at[zz])
 
         @pl.when(zz >= 6)
@@ -316,50 +330,54 @@
 
     lax.fori_loop(0, NZ, step, 0)
 
-    ox = []
+    def st_copy(d):
+        xx = (x + d) % NX
+        return remote(st_out.at[xx], sb.at[d], st_send.at[d], st_recv.at[d], z * NX + xx, t)
+
+    def o_copy(i, d):
+        xx = (x + d) % NX
+        return remote(
+            o_out.at[xx, i], ob.at[d, i], ox_send.at[4 * i + d], ox_recv.at[4 * i + d], z * NX + xx, t
+        )
+
     for d in (2, 1, 3, 0):
         xx = (x + d) % NX
         amount = jnp.sum(total[xx], axis=1, keepdims=True)
-        o_out[xx] = (mixed[xx] / amount).astype(BF16)
+        o_out[xx] = (mixed[xx] / amount).astype(BF16).reshape(4, 64, HD)
         st_out[xx] = (top[xx] + jnp.log2(amount)).T[:8, :]
         if d:
-            for i, (src, dst) in enumerate(((st_out, sb), (o_out, ob))):
-                copy = remote(
-                    src.at[xx], dst.at[d], ox_send.at[2 * d + i], ox_recv.at[2 * d + i], z * NX + xx, t
-                )
-                copy.start()
-                ox.append(copy)
+            st_copy(d).start()
+            o_copy(z % 4, d).start()
+    for j in range(1, 4):
+        for d in (2, 1, 3):
+            o_copy((z + j) % 4, d).start()
     for d in range(1, NX):
-        ref = wv.at[c, (x + NX - d) % NX]
-        arrived(ref, w_recv.at[d])
-        copy = remote(ref, ref, wc_send.at[d], wc_recv, ctx, partner)
-        copy.start()
-        wc.append(copy)
-    for d in range(1, NX):
-        arrived(sb.at[d], ox_recv.at[2 * d])
+        arrived(sb.at[d], st_recv.at[d])
     levels = [st_out[x]] + [sb[d] for d in range(1, NX)]
     best = jnp.maximum(jnp.maximum(levels[0], levels[1]), jnp.maximum(levels[2], levels[3]))
     parts = [jnp.exp2(level - best) for level in levels]
     amount = (parts[0] + parts[1]) + (parts[2] + parts[3])
     parts = [p / amount for p in parts]
-    table = jnp.concatenate(parts + [jnp.zeros((96, 256), F32)], axis=0).T
-    for d in range(1, NX):
-        arrived(ob.at[d], ox_recv.at[2 * d + 1])
-    joined = table[:, 0:1] * o_out[x].astype(F32)
-    for d in range(1, NX):
-        joined = joined + table[:, 8 * d : 8 * d + 1] * ob[d].astype(F32)
-    joined = joined.astype(BF16)
-    for i in range(4):
-        ab[i, y] = joined[64 * i : 64 * i + 64, :]
+    share_of[...] = jnp.concatenate(parts + [jnp.zeros((96, 256), F32)], axis=0).T
 
     def a_copy(i, d):
         ref = ab.at[i, y]
         return remote(ref, ref, a_send.at[8 * i + d], a_recv.at[i], ctx, 2 * ((y + d) % NY) + c)
 
     for j in range(4):
+        i = (z + j) % 4
+        part_share = share_of[aligned(64 * i, 64), :]
+        joined = part_share[:, 0:1] * o_out[x, i].astype(F32)
+        for d in range(1, NX):
+            arrived(ob.at[d, i], ox_recv.at[4 * i + d])
+            joined = joined + part_share[:, 8 * d : 8 * d + 1] * ob[d, i].astype(F32)
+        ab[i, y] = joined.astype(BF16)
         for d in (4, 3, 5, 2, 6, 1, 7):
-            a_copy((z + j) % 4, d).start()
-
+            a_copy(i, d).start()
+
+    for h in range(2):
+        arrived(wv.at[c, (x + 2) % NX, pl.ds(128 * h, 128)], w_recv.at[2 * h])
+    w_core(2).start()
     arrived(wv.at[0], wc_recv)
     w_own.wait()
 
@@ -399,8 +417,15 @@
         copy.start()
     pltpu.make_async_copy(fb.at[t], fr.at[t], f_recv).start()
 
-    for copy in q1 + q2 + kz + qx + wx + wc + ox:
+    for copy in q1 + q2 + kz + qx + wx + wc:
         copy.wait_send()
+    for d in range(1, NX):
+        w_core(d).wait_send()
+        st_copy(d).wait_send()
+        for i in range(4):
+            o_copy(i, d).wait_send()
+    for d in (1, 3):
+        w_relay(d).wait_send()
 
     def sent(zz, carry):
         for kv in range(2):
@@ -456,10 +481,11 @@
             vmem((NX, 256, 128), F32),
             vmem((NX, 256, 128), F32),
             vmem((NX, 256, HD), F32),
-            vmem((NX, 256, HD), BF16),
+            vmem((NX, 4, 64, HD), BF16),
             vmem((NX, 8, 256), F32),
-            vmem((NX, 256, HD), BF16),
+            vmem((NX, 4, 64, HD), BF16),
             vmem((NX, 8, 256), F32),
+            vmem((256, 128), F32),
             vmem((4, NY, 64, HD), BF16),
             vmem((4, 2, 64, 512), BF16),
             vmem((NZ, 64, 512), BF16),
@@ -468,7 +494,7 @@
             dma((21,)),
             dma((8,)), dma, dma((16,)), dma, dma((4,)), dma((4,)),
             dma((16,)), dma((16,)), dma((16,)), dma((16,)), dma((32,)), dma((8,)),
-            dma((4,)), dma((4,)), dma((4,)), dma, dma((8,)), dma((8,)),
+            dma((4,)), dma((4,)), dma((4,)), dma, dma((4,)), dma((4,)), dma((16,)), dma((16,)),
             dma((32,)), dma((4,)), dma((8,)), dma, dma((16,)), dma,
         ],
         compiler_params=pltpu.CompilerParams(

time: 77.5 us -> 76.2 us (0.983)
  Pallas kernels: 75.8 us -> 73.7 us
    pallas_call x1, Pallas kernels: 75.8 us -> 73.7 us  [layer(): pl.pallas_call(layer_kernel, out_shape=jax.ShapeDtypeStruct((4, 8192), BF...]
where the time goes in v5:
time: 76.2 us; the launch traced here: 75.2 us
  Pallas kernels  73.7 us (97%)
  local copies, waits for them, and re-layouts  1.49 us (2%)
    pallas_call x1, Pallas kernels, layer(): pl.pallas_call(layer_kernel, out_shape=jax.ShapeDtypeStruct((4, 8192), BF...  73.7 us

profile of v5, /device:TPU:1, one launch (start us, length us, event | category | flops | bytes accessed | tf_op | source)
XLA Modules:
  0.0 75.2 jit_solution(16882325216986662198)
XLA Ops:
  0.0 73.7 %layer.1 = bf16[4,8192]{1,0:T(4,128)(2,1)} custom-call(bf16[4,8192]{1,0:T(4,128)(2,1)} %q_ref.1, bf16[512,1024]{1,0:T(8,128)(2,1)} %k_ref.1, bf16[512,1024]{1,0:T(8,128)(2,1)} %v_ref.1, bf16[256,512]{1,0:T(8,128)(2,1)} %w_ref.1, s32[64]{0:T(128)} %kind_ref.1, s32[64]{0:T(128)} %count_ref.1, s32[32,16,64]{2,1,0:T(8,128)} %bitcast.1, s32[64,1024]{1,0:T(8,128)} %cols_ref.1, ...), custom_call_target="tpu_custom_call" | custom-call | tf_op jit(solution)/shard_map/layer/pallas_call | solution.py:460
  73.7 1.5 %copy.11 = bf16[4,8192]{1,0:T(4,128)(2,1)} copy(bf16[4,8192]{1,0:T(4,128)(2,1)} %layer.1) | data formatting | bytes 131072

commit v6 on v5

--- a/solution.py
+++ b/solution.py
@@ -101,11 +101,11 @@
     q_ref, k_ref, v_ref, w_ref, kind_ref, count_ref, blocks_ref, cols_ref, offs_ref,
     out_ref,
     qv, qt, qs, qy, q4, qf, qb, kl, kvb, wv, blocks, cols8, offs8, row_bias, tile_bias,
-    top, total, mixed, o_out, st_out, ob, sb, share_of, ab, part, rb, fb, fr,
+    top, total, mixed, o_out, st_out, ob, sb, share_of, ab, part, rb,
     in_sem, q1_send, q1_recv, q2_send, q2_recv, qx_send, qx_recv,
     kz_send, kz_recv, ky_send, ky_recv, kc_send, kc_recv,
     w_send, w_recv, wc_send, wc_recv, st_send, st_recv, ox_send, ox_recv,
-    a_send, a_recv, z_send, z_recv, f_send, f_recv,
+    a_send, a_recv, z_send, z_recv,
 ):
     ctx = lax.axis_index("ctx")
     t = lax.axis_index("tp")
@@ -381,9 +381,10 @@
     arrived(wv.at[0], wc_recv)
     w_own.wait()
 
-    def z_copy(i, cc):
+    def z_copy(i, d):
+        tt = (t + d) % NT
         return remote(
-            part.at[i, cc], rb.at[z], z_send.at[2 * i + cc], z_recv, (4 * c + i) * NX + x, 2 * y + cc
+            part.at[i, tt], rb.at[z, y], z_send.at[NT * i + d], z_recv, (4 * c + i) * NX + x, tt
         )
 
     for j in range(4):
@@ -392,30 +393,19 @@
         features = jnp.concatenate([ab[i, yy] for yy in range(NY)], axis=1)
         for cc in range(2):
             weight = wv[cc].reshape(1024, 512)
-            part[i, cc] = jnp.dot(features, weight, preferred_element_type=F32).astype(BF16)
-            mine = jnp.logical_and(4 * c + i == z, cc == c)
-
-            @pl.when(jnp.logical_not(mine))
-            def _():
-                z_copy(i, cc).start()
-
-            @pl.when(mine)
-            def _():
-                pltpu.make_async_copy(part.at[i, cc], rb.at[z], z_recv).start()
-
-    arrived(rb, z_recv)
-    summed = rb[0].astype(F32)
-    for g in range(1, NZ):
-        summed = summed + rb[g].astype(F32)
-    for tt in range(NT):
-        fb[tt] = summed[4 * tt : 4 * tt + 4, :].astype(BF16)
-    last = [
-        remote(fb.at[(t + d) % NT], fr.at[t], f_send.at[d], f_recv, ctx, (t + d) % NT)
-        for d in range(1, NT)
-    ]
-    for copy in last:
-        copy.start()
-    pltpu.make_async_copy(fb.at[t], fr.at[t], f_recv).start()
+            rows = jnp.dot(features, weight, preferred_element_type=F32)
+            for tt in range(NT):
+                part[i, tt, :, 512 * cc : 512 * cc + 512] = rows[4 * tt : 4 * tt + 4, :].astype(BF16)
+        for d in range(1, NT):
+            z_copy(i, d).start()
+
+        @pl.when(4 * c + i == z)
+        def _():
+            pltpu.make_async_copy(part.at[i, t], rb.at[z, y], z_recv).start()
+
+        @pl.when(4 * c + i != z)
+        def _():
+            z_copy(i, 0).start()
 
     for copy in q1 + q2 + kz + qx + wx + wc:
         copy.wait_send()
@@ -438,18 +428,19 @@
     for i in range(4):
         for d in range(1, NY):
             a_copy(i, d).wait_send()
-        for cc in range(2):
-            mine = jnp.logical_and(4 * c + i == z, cc == c)
-
-            @pl.when(jnp.logical_not(mine))
-            def _():
-                z_copy(i, cc).wait_send()
-
-    arrived(fr, f_recv)
-    for tt in range(NT):
-        out_ref[:, 512 * tt : 512 * tt + 512] = fr[tt]
-    for copy in last:
-        copy.wait_send()
+        for d in range(1, NT):
+            z_copy(i, d).wait_send()
+
+        @pl.when(4 * c + i != z)
+        def _():
+            z_copy(i, 0).wait_send()
+
+    arrived(rb, z_recv)
+    for yy in range(NY):
+        summed = rb[0, yy].astype(F32)
+        for g in range(1, NZ):
+            summed = summed + rb[g, yy].astype(F32)
+        out_ref[:, 1024 * yy : 1024 * yy + 1024] = summed.astype(BF16)
 
 
 def layer(q, k, v, w, kinds, counts, blocks, cols, offs):
@@ -487,15 +478,13 @@
             vmem((NX, 8, 256), F32),
             vmem((256, 128), F32),
             vmem((4, NY, 64, HD), BF16),
-            vmem((4, 2, 64, 512), BF16),
-            vmem((NZ, 64, 512), BF16),
-            vmem((NT, 4, 512), BF16),
-            vmem((NT, 4, 512), BF16),
+            vmem((4, NT, 4, 1024), BF16),
+            vmem((NZ, NY, 4, 1024), BF16),
             dma((21,)),
             dma((8,)), dma, dma((16,)), dma, dma((4,)), dma((4,)),
             dma((16,)), dma((16,)), dma((16,)), dma((16,)), dma((32,)), dma((8,)),
             dma((4,)), dma((4,)), dma((4,)), dma, dma((4,)), dma((4,)), dma((16,)), dma((16,)),
-            dma((32,)), dma((4,)), dma((8,)), dma, dma((16,)), dma,
+            dma((32,)), dma((4,)), dma((64,)), dma,
         ],
         compiler_params=pltpu.CompilerParams(
             collective_id=0, has_side_effects=True, vmem_limit_bytes=56 * 1024 * 1024

time: 76.2 us -> 77.8 us (1.021); the launches traced: 75.2 us -> 77.6 us
  Pallas kernels: 73.7 us -> 76.1 us
    pallas_call x1, Pallas kernels: 73.7 us -> 76.1 us  [layer(): pl.pallas_call(layer_kernel, out_shape=jax.ShapeDtypeStruct((4, 8192), BF...]
where the time goes in v6:
time: 77.8 us; the launch traced here: 77.6 us
  Pallas kernels  76.1 us (98%)
  local copies, waits for them, and re-layouts  1.49 us (2%)
    pallas_call x1, Pallas kernels, layer(): pl.pallas_call(layer_kernel, out_shape=jax.ShapeDtypeStruct((4, 8192), BF...  76.1 us

profile of v6, /device:TPU:1, one launch (start us, length us, event | category | flops | bytes accessed | tf_op | source)
XLA Modules:
  0.0 77.6 jit_solution(3275228052671222415)
XLA Ops:
  0.0 76.1 %layer.1 = bf16[4,8192]{1,0:T(4,128)(2,1)} custom-call(bf16[4,8192]{1,0:T(4,128)(2,1)} %q_ref.1, bf16[512,1024]{1,0:T(8,128)(2,1)} %k_ref.1, bf16[512,1024]{1,0:T(8,128)(2,1)} %v_ref.1, bf16[256,512]{1,0:T(8,128)(2,1)} %w_ref.1, s32[64]{0:T(128)} %kind_ref.1, s32[64]{0:T(128)} %count_ref.1, s32[32,16,64]{2,1,0:T(8,128)} %bitcast.1, s32[64,1024]{1,0:T(8,128)} %cols_ref.1, ...), custom_call_target="tpu_custom_call" | custom-call | tf_op jit(solution)/shard_map/layer/pallas_call | solution.py:451
  76.1 1.5 %copy.11 = bf16[4,8192]{1,0:T(4,128)(2,1)} copy(bf16[4,8192]{1,0:T(4,128)(2,1)} %layer.1) | data formatting | bytes 131072

commit v7 on v5

--- a/solution.py
+++ b/solution.py
@@ -101,11 +101,11 @@
     q_ref, k_ref, v_ref, w_ref, kind_ref, count_ref, blocks_ref, cols_ref, offs_ref,
     out_ref,
     qv, qt, qs, qy, q4, qf, qb, kl, kvb, wv, blocks, cols8, offs8, row_bias, tile_bias,
-    top, total, mixed, o_out, st_out, ob, sb, share_of, ab, part, rb, fb, fr,
+    top, total, mixed, o_out, st_out, ob, sb, share_of, ab, part, early, pieces, late, fb, fr,
     in_sem, q1_send, q1_recv, q2_send, q2_recv, qx_send, qx_recv,
     kz_send, kz_recv, ky_send, ky_recv, kc_send, kc_recv,
     w_send, w_recv, wc_send, wc_recv, st_send, st_recv, ox_send, ox_recv,
-    a_send, a_recv, z_send, z_recv, f_send, f_recv,
+    a_send, a_recv, z_send, z_recv, r_send, r_recv, f_send, f_recv,
 ):
     ctx = lax.axis_index("ctx")
     t = lax.axis_index("tp")
@@ -381,9 +381,18 @@
     arrived(wv.at[0], wc_recv)
     w_own.wait()
 
-    def z_copy(i, cc):
+    def z_copy(j, cc):
+        to = (4 * c + (z + j) % 4) * NX + x
         return remote(
-            part.at[i, cc], rb.at[z], z_send.at[2 * i + cc], z_recv, (4 * c + i) * NX + x, 2 * y + cc
+            part.at[j, cc], early.at[2 * j + z // 4], z_send.at[2 * j + cc], z_recv, to, 2 * y + cc
+        )
+
+    def row_copy(j, d):
+        to = (4 * c + (z + j) % 4) * NX + x
+        tt = (t + d) % NT
+        return remote(
+            pieces.at[j - 2, tt], late.at[2 * (j - 2) + z // 4, y],
+            r_send.at[NT * (j - 2) + d], r_recv, to, tt,
         )
 
     for j in range(4):
@@ -392,21 +401,31 @@
         features = jnp.concatenate([ab[i, yy] for yy in range(NY)], axis=1)
         for cc in range(2):
             weight = wv[cc].reshape(1024, 512)
-            part[i, cc] = jnp.dot(features, weight, preferred_element_type=F32).astype(BF16)
+            rows = jnp.dot(features, weight, preferred_element_type=F32)
+            if j >= 2:
+                for tt in range(NT):
+                    pieces[j - 2, tt, :, 512 * cc : 512 * cc + 512] = rows[4 * tt : 4 * tt + 4, :].astype(BF16)
+                continue
+            part[j, cc] = rows.astype(BF16)
+            if j:
+                z_copy(j, cc).start()
+                continue
             mine = jnp.logical_and(4 * c + i == z, cc == c)
 
             @pl.when(jnp.logical_not(mine))
             def _():
-                z_copy(i, cc).start()
+                z_copy(0, cc).start()
 
             @pl.when(mine)
             def _():
-                pltpu.make_async_copy(part.at[i, cc], rb.at[z], z_recv).start()
-
-    arrived(rb, z_recv)
-    summed = rb[0].astype(F32)
-    for g in range(1, NZ):
-        summed = summed + rb[g].astype(F32)
+                pltpu.make_async_copy(part.at[0, cc], early.at[z // 4], z_recv).start()
+
+        if j >= 2:
+            for d in range(NT):
+                row_copy(j, d).start()
+
+    arrived(early, z_recv)
+    summed = (early[0].astype(F32) + early[1].astype(F32)) + (early[2].astype(F32) + early[3].astype(F32))
     for tt in range(NT):
         fb[tt] = summed[4 * tt : 4 * tt + 4, :].astype(BF16)
     last = [
@@ -438,18 +457,27 @@
     for i in range(4):
         for d in range(1, NY):
             a_copy(i, d).wait_send()
-        for cc in range(2):
-            mine = jnp.logical_and(4 * c + i == z, cc == c)
-
-            @pl.when(jnp.logical_not(mine))
-            def _():
-                z_copy(i, cc).wait_send()
-
+    for cc in range(2):
+        mine = jnp.logical_and(4 * c + z % 4 == z, cc == c)
+
+        @pl.when(jnp.logical_not(mine))
+        def _():
+            z_copy(0, cc).wait_send()
+
+        z_copy(1, cc).wait_send()
+    for j in (2, 3):
+        for d in range(NT):
+            row_copy(j, d).wait_send()
+    for copy in last:
+        copy.wait_send()
+
+    arrived(late, r_recv)
     arrived(fr, f_recv)
     for tt in range(NT):
-        out_ref[:, 512 * tt : 512 * tt + 512] = fr[tt]
-    for copy in last:
-        copy.wait_send()
+        summed = fr[tt].astype(F32)
+        for e in range(4):
+            summed = summed + late[e, tt // 2, :, 512 * (tt % 2) : 512 * (tt % 2) + 512].astype(F32)
+        out_ref[:, 512 * tt : 512 * tt + 512] = summed.astype(BF16)
 
 
 def layer(q, k, v, w, kinds, counts, blocks, cols, offs):
@@ -487,18 +515,20 @@
             vmem((NX, 8, 256), F32),
             vmem((256, 128), F32),
             vmem((4, NY, 64, HD), BF16),
-            vmem((4, 2, 64, 512), BF16),
-            vmem((NZ, 64, 512), BF16),
+            vmem((2, 2, 64, 512), BF16),
+            vmem((4, 64, 512), BF16),
+            vmem((2, NT, 4, 1024), BF16),
+            vmem((4, NY, 4, 1024), BF16),
             vmem((NT, 4, 512), BF16),
             vmem((NT, 4, 512), BF16),
             dma((21,)),
             dma((8,)), dma, dma((16,)), dma, dma((4,)), dma((4,)),
             dma((16,)), dma((16,)), dma((16,)), dma((16,)), dma((32,)), dma((8,)),
             dma((4,)), dma((4,)), dma((4,)), dma, dma((4,)), dma((4,)), dma((16,)), dma((16,)),
-            dma((32,)), dma((4,)), dma((8,)), dma, dma((16,)), dma,
+            dma((32,)), dma((4,)), dma((4,)), dma, dma((32,)), dma, dma((16,)), dma,
         ],
         compiler_params=pltpu.CompilerParams(
-            collective_id=0, has_side_effects=True, vmem_limit_bytes=56 * 1024 * 1024
+            collective_id=0, has_side_effects=True, vmem_limit_bytes=56_450_000
         ),
         name="layer",
     )(q, k, v, w, kinds, counts, blocks, cols, offs)

time: 76.2 us -> 76.6 us (level); the launches traced: 75.2 us -> 76.4 us
    unnamed x1 -> x7, local copies, waits for them, and re-layouts: 1.49 us -> 2.06 us
where the time goes in v7:
time: 76.6 us; the launch traced here: 76.4 us
  Pallas kernels  74.3 us (97%)
  local copies, waits for them, and re-layouts  2.06 us (3%)
    pallas_call x1, Pallas kernels, layer(): pl.pallas_call(layer_kernel, out_shape=jax.ShapeDtypeStruct((4, 8192), BF...  74.3 us
    unnamed x7, local copies, waits for them, and re-layouts  2.06 us

profile of v7, /device:TPU:1, one launch (start us, length us, event | category | flops | bytes accessed | tf_op | source)
XLA Modules:
  0.0 76.4 jit_solution(1629804094724703282)
XLA Ops:
  0.0 0.0 copy-start.2
  0.0 0.0 copy-start.1
  0.0 0.7 copy-done.2
  0.7 0.0 copy-done.1
  0.7 0.0 copy-start
  0.7 0.8 copy-done
  1.4 74.3 %layer.1 = bf16[4,8192]{1,0:T(4,128)(2,1)S(1)} custom-call(bf16[4,8192]{1,0:T(4,128)(2,1)} %q_ref.1, bf16[512,1024]{1,0:T(8,128)(2,1)} %k_ref.1, bf16[512,1024]{1,0:T(8,128)(2,1)} %v_ref.1, bf16[256,512]{1,0:T(8,128)(2,1)} %w_ref.1, s32[64]{0:T(128)S(1)} %copy-done.1, s32[64]{0:T(128)S(1)} %copy-done.2, s32[32,16,64]{2,1,0:T(8,128)} %bitcast.1, ...), custom_call_target="tpu_custom_call" | custom-call | tf_op jit(solution)/shard_map/layer/pallas_call | solution.py:488
  75.7 0.6 copy.11
Async XLA Ops:
  0.0 0.7 copy-start.2
  0.0 0.7 copy-start.1
  0.7 0.8 copy-start

commit v8 on v7

--- a/solution.py
+++ b/solution.py
@@ -259,23 +259,17 @@
         ref = wv.at[c, (x + NX - d) % NX]
         return remote(ref, ref, wc_send.at[d], wc_recv, ctx, partner)
 
-    for i in range(3, 7):
-        forward_own(i)
-        forward_other(i - 2)
-    for d in range(1, NX):
-        arrived(qb.at[(x + NX - d) % NX], qx_recv.at[d])
-    forward_own(7)
-
-    def chunk(zz, band):
+    def chunk(zz, band, groups):
         keys = kvb[zz, 0]
         values = kvb[zz, 1]
 
-        queries = qb[...].reshape(1024, HD)
+        queries = [qb[(x + k) % NX].reshape(256, HD) for k in groups]
+        queries = queries[0] if len(queries) == 1 else jnp.concatenate(queries, axis=0)
         s = lax.dot_general(queries, keys, (((1,), (1,)), ((), ())), preferred_element_type=F32)
         weights = []
         factors = []
-        for n in range(16):
-            xx, zl = n // 4, n % 4
+        for n in range(4 * len(groups)):
+            xx, zl = (x + groups[n // 4]) % NX, n % 4
             b = 16 * c + 4 * zl + xx
             old = top[xx, 64 * zl : 64 * zl + 64]
             tiles = []
@@ -298,37 +292,56 @@
             factors.append(factor)
             weights.append(jnp.concatenate([tile.astype(BF16) for tile in tiles], axis=1))
         added = jnp.dot(jnp.concatenate(weights, axis=0), values, preferred_element_type=F32)
-        for n in range(16):
-            at = (n // 4, pl.ds(64 * (n % 4), 64))
+        for n in range(4 * len(groups)):
+            at = ((x + groups[n // 4]) % NX, pl.ds(64 * (n % 4), 64))
             mixed[at] = mixed[at] * factors[n] + added[64 * n : 64 * n + 64]
 
-    def step(i, carry):
+    def attend(zz, groups):
+        @pl.when(zz >= 6)
+        def _():
+            chunk(zz, True, groups)
+
+        @pl.when(zz < 6)
+        def _():
+            chunk(zz, False, groups)
+
+    def own_step(i, carry):
         zz = (z + by_distance(i)) % NZ
 
-        @pl.when(i < NZ - 5)
+        @pl.when(i < NZ - 3)
         def _():
-            forward_other(i + 5)
-
-        @pl.when(i == 5)
+            forward_own(i + 3)
+
+        forward_other(i + 1)
+        arrived(kvb.at[zz, 0], kc_recv.at[zz])
+        attend(zz, (0,))
+        return carry
+
+    lax.fori_loop(0, 6, own_step, 0)
+    forward_other(7)
+    for d in range(1, NX):
+        arrived(qb.at[(x + NX - d) % NX], qx_recv.at[d])
+
+    def rest_step(i, carry):
+        @pl.when(i == 3)
         def _():
             for d in (1, 3):
                 arrived(wv.at[c, (x + NX - d) % NX], w_recv.at[d])
                 w_relay(d).start()
                 w_core(d).start()
 
+        attend((z + by_distance(i)) % NZ, (1, 2, 3))
+        return carry
+
+    lax.fori_loop(0, 6, rest_step, 0)
+
+    def late_step(i, carry):
+        zz = (z + by_distance(i)) % NZ
         arrived(kvb.at[zz, 0], kc_recv.at[zz])
-
-        @pl.when(zz >= 6)
-        def _():
-            chunk(zz, True)
-
-        @pl.when(zz < 6)
-        def _():
-            chunk(zz, False)
-
+        attend(zz, (0, 1, 2, 3))
         return carry
 
-    lax.fori_loop(0, NZ, step, 0)
+    lax.fori_loop(6, NZ, late_step, 0)
 
     def st_copy(d):
         xx = (x + d) % NX
@@ -528,7 +541,7 @@
             dma((32,)), dma((4,)), dma((4,)), dma, dma((32,)), dma, dma((16,)), dma,
         ],
         compiler_params=pltpu.CompilerParams(
-            collective_id=0, has_side_effects=True, vmem_limit_bytes=56_450_000
+            collective_id=0, has_side_effects=True, vmem_limit_bytes=56 * 1024 * 1024
         ),
         name="layer",
     )(q, k, v, w, kinds, counts, blocks, cols, offs)

time: 76.6 us -> 77.5 us (1.012)
  Pallas kernels: 74.3 us -> 75.8 us
    pallas_call x1, Pallas kernels: 74.3 us -> 75.8 us  [layer(): pl.pallas_call(layer_kernel, out_shape=jax.ShapeDtypeStruct((4, 8192), BF...]
    unnamed x7 -> x1, local copies, waits for them, and re-layouts: 2.06 us -> 1.49 us
where the time goes in v8:
time: 77.5 us; the launch traced here: 77.3 us
  Pallas kernels  75.8 us (98%)
  local copies, waits for them, and re-layouts  1.49 us (2%)
    pallas_call x1, Pallas kernels, layer(): pl.pallas_call(layer_kernel, out_shape=jax.ShapeDtypeStruct((4, 8192), BF...  75.8 us

profile of v8, /device:TPU:1, one launch (start us, length us, event | category | flops | bytes accessed | tf_op | source)
XLA Modules:
  0.0 77.3 jit_solution(10652961144595860952)
XLA Ops:
  0.0 75.8 %layer.1 = bf16[4,8192]{1,0:T(4,128)(2,1)} custom-call(bf16[4,8192]{1,0:T(4,128)(2,1)} %q_ref.1, bf16[512,1024]{1,0:T(8,128)(2,1)} %k_ref.1, bf16[512,1024]{1,0:T(8,128)(2,1)} %v_ref.1, bf16[256,512]{1,0:T(8,128)(2,1)} %w_ref.1, s32[64]{0:T(128)} %kind_ref.1, s32[64]{0:T(128)} %count_ref.1, s32[32,16,64]{2,1,0:T(8,128)} %bitcast.1, s32[64,1024]{1,0:T(8,128)} %cols_ref.1, ...), custom_call_target="tpu_custom_call" | custom-call | tf_op jit(solution)/shard_map/layer/pallas_call | solution.py:501
  75.8 1.5 %copy.11 = bf16[4,8192]{1,0:T(4,128)(2,1)} copy(bf16[4,8192]{1,0:T(4,128)(2,1)} %layer.1) | data formatting | bytes 131072

commit v9 on v7

--- a/solution.py
+++ b/solution.py
@@ -119,27 +119,21 @@
         pltpu.make_async_copy(cols_ref.at[aligned(8 * z, 8)], cols8, in_sem.at[2]),
         pltpu.make_async_copy(offs_ref.at[aligned(8 * z, 8)], offs8, in_sem.at[3]),
     ]
+    barrier = pltpu.get_barrier_semaphore()
+
+    def greet(to_ctx, to_tp):
+        pl.semaphore_signal(barrier, inc=1, device_id=(to_ctx, to_tp), device_id_type=MESH)
+
+    for d in (4, 3, 5, 2, 6, 1, 7):
+        greet(((z + d) % NZ) * NX + x, t)
+        for core in (c, 1 - c):
+            greet(ctx, 2 * ((y + d) % NY) + core)
+    for d in (2, 1, 3):
+        greet(z * NX + (x + d) % NX, t)
+    greet(ctx, partner)
+
     for copy in loads:
         copy.start()
-
-    barrier = pltpu.get_barrier_semaphore()
-
-    def greet(to_ctx, to_tp):
-        pl.semaphore_signal(barrier, inc=1, device_id=(to_ctx, to_tp), device_id_type=MESH)
-
-    for d in range(1, NT):
-        greet(ctx, (t + d) % NT)
-    for d in range(1, NZ):
-        for cc in range(2):
-            greet(((z + d) % NZ) * NX + x, 2 * y + cc)
-    for d in range(1, NX):
-        greet(z * NX + (x + d) % NX, t)
-
-    loads[0].wait()
-    for yy in range(NY):
-        for g in range(KVH):
-            at = (8 * g + yy) * HD
-            qt[g, yy] = qv[:, at : at + HD]
     share = 2 * (y % 2) + c
     other = 2 * (1 - y % 2) + c
 
@@ -159,9 +153,14 @@
     w_own = pltpu.make_async_copy(w_ref, wv.at[c, x], in_sem.at[4])
     w_own.start()
 
+    loads[0].wait()
+    for yy in range(NY):
+        for g in range(KVH):
+            at = (8 * g + yy) * HD
+            qt[g, yy] = qv[:, at : at + HD]
     for copy in dense:
         copy.wait()
-    pl.semaphore_wait(barrier, NT - 1 + 2 * (NZ - 1) + NX - 1)
+    pl.semaphore_wait(barrier, NT - 1 + NZ - 1 + NX - 1)
 
     q1 = [
         remote(qt.at[(z + d) % NZ], qs.at[z], q1_send.at[d], q1_recv, ((z + d) % NZ) * NX + x, t)
@@ -227,10 +226,6 @@
         q2[-1].start()
     pltpu.make_async_copy(qy.at[y, pl.ds(4 * c, 4)], q4.at[t], q2_recv).start()
 
-    forward_own(1)
-    forward_own(2)
-    forward_other(0)
-
     arrived(q4, q2_recv)
     for zl in range(4):
         for tt in range(NT):
@@ -259,12 +254,15 @@
         ref = wv.at[c, (x + NX - d) % NX]
         return remote(ref, ref, wc_send.at[d], wc_recv, ctx, partner)
 
-    for i in range(3, 7):
+    forward_other(0)
+    for i in range(1, 6):
         forward_own(i)
-        forward_other(i - 2)
     for d in range(1, NX):
         arrived(qb.at[(x + NX - d) % NX], qx_recv.at[d])
+    forward_own(6)
+    forward_other(1)
     forward_own(7)
+    forward_other(2)
 
     def chunk(zz, band):
         keys = kvb[zz, 0]
@@ -305,9 +303,9 @@
     def step(i, carry):
         zz = (z + by_distance(i)) % NZ
 
-        @pl.when(i < NZ - 5)
+        @pl.when(i < NZ - 3)
         def _():
-            forward_other(i + 5)
+            forward_other(i + 3)
 
         @pl.when(i == 5)
         def _():
@@ -528,7 +526,7 @@
             dma((32,)), dma((4,)), dma((4,)), dma, dma((32,)), dma, dma((16,)), dma,
         ],
         compiler_params=pltpu.CompilerParams(
-            collective_id=0, has_side_effects=True, vmem_limit_bytes=56_450_000
+            collective_id=0, has_side_effects=True, vmem_limit_bytes=56 * 1024 * 1024
         ),
         name="layer",
     )(q, k, v, w, kinds, counts, blocks, cols, offs)

time: 76.6 us -> 75.6 us (0.987)
    unnamed x7 -> x1, local copies, waits for them, and re-layouts: 2.06 us -> 1.49 us
where the time goes in v9:
time: 75.6 us; the launch traced here: 75.4 us
  Pallas kernels  73.9 us (98%)
  local copies, waits for them, and re-layouts  1.49 us (2%)
    pallas_call x1, Pallas kernels, layer(): pl.pallas_call(layer_kernel, out_shape=jax.ShapeDtypeStruct((4, 8192), BF...  73.9 us

profile of v9, /device:TPU:1, one launch (start us, length us, event | category | flops | bytes accessed | tf_op | source)
XLA Modules:
  0.0 75.4 jit_solution(9401672170995616371)
XLA Ops:
  0.0 73.9 %layer.1 = bf16[4,8192]{1,0:T(4,128)(2,1)} custom-call(bf16[4,8192]{1,0:T(4,128)(2,1)} %q_ref.1, bf16[512,1024]{1,0:T(8,128)(2,1)} %k_ref.1, bf16[512,1024]{1,0:T(8,128)(2,1)} %v_ref.1, bf16[256,512]{1,0:T(8,128)(2,1)} %w_ref.1, s32[64]{0:T(128)} %kind_ref.1, s32[64]{0:T(128)} %count_ref.1, s32[32,16,64]{2,1,0:T(8,128)} %bitcast.1, s32[64,1024]{1,0:T(8,128)} %cols_ref.1, ...), custom_call_target="tpu_custom_call" | custom-call | tf_op jit(solution)/shard_map/layer/pallas_call | solution.py:486
  73.9 1.5 %copy.11 = bf16[4,8192]{1,0:T(4,128)(2,1)} copy(bf16[4,8192]{1,0:T(4,128)(2,1)} %layer.1) | data formatting | bytes 131072

commit v10 on v9

--- a/solution.py
+++ b/solution.py
@@ -338,17 +338,26 @@
             o_out.at[xx, i], ob.at[d, i], ox_send.at[4 * i + d], ox_recv.at[4 * i + d], z * NX + xx, t
         )
 
+    def divide(d, i):
+        xx = (x + d) % NX
+        at = (xx, aligned(64 * i, 64))
+        o_out[xx, i] = (mixed[at] * total[at]).astype(BF16)
+
     for d in (2, 1, 3, 0):
         xx = (x + d) % NX
         amount = jnp.sum(total[xx], axis=1, keepdims=True)
-        o_out[xx] = (mixed[xx] / amount).astype(BF16).reshape(4, 64, HD)
+        total[xx] = jnp.broadcast_to(1.0 / amount, (256, 128))
         st_out[xx] = (top[xx] + jnp.log2(amount)).T[:8, :]
         if d:
             st_copy(d).start()
+            divide(d, z % 4)
             o_copy(z % 4, d).start()
     for j in range(1, 4):
         for d in (2, 1, 3):
+            divide(d, (z + j) % 4)
             o_copy((z + j) % 4, d).start()
+    for i in range(4):
+        divide(0, i)
     for d in range(1, NX):
         arrived(sb.at[d], st_recv.at[d])
     levels = [st_out[x]] + [sb[d] for d in range(1, NX)]

time: 75.6 us -> 75.5 us (level)
  no operation moved by 1% of the time
where the time goes in v10:
time: 75.5 us; the launch traced here: 75.3 us
  Pallas kernels  73.8 us (98%)
  local copies, waits for them, and re-layouts  1.49 us (2%)
    pallas_call x1, Pallas kernels, layer(): pl.pallas_call(layer_kernel, out_shape=jax.ShapeDtypeStruct((4, 8192), BF...  73.8 us

profile of v10, /device:TPU:1, one launch (start us, length us, event | category | flops | bytes accessed | tf_op | source)
XLA Modules:
  0.0 75.3 jit_solution(12696504392619818986)
XLA Ops:
  0.0 73.8 %layer.1 = bf16[4,8192]{1,0:T(4,128)(2,1)} custom-call(bf16[4,8192]{1,0:T(4,128)(2,1)} %q_ref.1, bf16[512,1024]{1,0:T(8,128)(2,1)} %k_ref.1, bf16[512,1024]{1,0:T(8,128)(2,1)} %v_ref.1, bf16[256,512]{1,0:T(8,128)(2,1)} %w_ref.1, s32[64]{0:T(128)} %kind_ref.1, s32[64]{0:T(128)} %count_ref.1, s32[32,16,64]{2,1,0:T(8,128)} %bitcast.1, s32[64,1024]{1,0:T(8,128)} %cols_ref.1, ...), custom_call_target="tpu_custom_call" | custom-call | tf_op jit(solution)/shard_map/layer/pallas_call | solution.py:495
  73.8 1.5 %copy.11 = bf16[4,8192]{1,0:T(4,128)(2,1)} copy(bf16[4,8192]{1,0:T(4,128)(2,1)} %layer.1) | data formatting | bytes 131072

commit v11 on v10

--- a/solution.py
+++ b/solution.py
@@ -98,9 +98,9 @@
 
 
 def layer_kernel(
-    q_ref, k_ref, v_ref, w_ref, kind_ref, count_ref, blocks_ref, cols_ref, offs_ref,
+    q_ref, k_ref, v_ref, w_ref, kinds_ref, counts_ref, blocks_ref, cols_ref, offs_ref,
     out_ref,
-    qv, qt, qs, qy, q4, qf, qb, kl, kvb, wv, blocks, cols8, offs8, row_bias, tile_bias,
+    qv, qt, qs, qy, q4, qf, qb, kl, kvb, wv, kind_ref, count_ref, blocks, cols8, offs8, row_bias, tile_bias,
     top, total, mixed, o_out, st_out, ob, sb, share_of, ab, part, early, pieces, late, fb, fr,
     in_sem, q1_send, q1_recv, q2_send, q2_recv, qx_send, qx_recv,
     kz_send, kz_recv, ky_send, ky_recv, kc_send, kc_recv,
@@ -118,6 +118,8 @@
         pltpu.make_async_copy(blocks_ref, blocks, in_sem.at[1]),
         pltpu.make_async_copy(cols_ref.at[aligned(8 * z, 8)], cols8, in_sem.at[2]),
         pltpu.make_async_copy(offs_ref.at[aligned(8 * z, 8)], offs8, in_sem.at[3]),
+        pltpu.make_async_copy(kinds_ref, kind_ref, in_sem.at[5]),
+        pltpu.make_async_copy(counts_ref, count_ref, in_sem.at[13]),
     ]
     barrier = pltpu.get_barrier_semaphore()
 
@@ -490,12 +492,11 @@
 def layer(q, k, v, w, kinds, counts, blocks, cols, offs):
     dma = pltpu.SemaphoreType.DMA
     hbm = pl.BlockSpec(memory_space=pltpu.HBM)
-    smem = pl.BlockSpec(memory_space=pltpu.SMEM)
     vmem = pltpu.VMEM
     return pl.pallas_call(
         layer_kernel,
         out_shape=jax.ShapeDtypeStruct((4, 8192), BF16),
-        in_specs=[hbm, hbm, hbm, hbm, smem, smem, hbm, hbm, hbm],
+        in_specs=[hbm] * 9,
         out_specs=pl.BlockSpec(memory_space=pltpu.VMEM),
         scratch_shapes=[
             vmem((4, 8192), BF16),
@@ -508,6 +509,8 @@
             vmem((2, NZ, 128, HD), BF16),
             vmem((NZ, 2, 512, HD), BF16),
             vmem((2, NX, 256, 512), BF16),
+            pltpu.SMEM((H,), jnp.int32),
+            pltpu.SMEM((H,), jnp.int32),
             vmem((32, 16, H), jnp.int32),
             vmem((8, 1024), jnp.int32),
             vmem((8, 128), jnp.int32),

time: 75.5 us -> 74.9 us (level)
  no operation moved by 1% of the time
where the time goes in v11:
time: 74.9 us; the launch traced here: 74.7 us
  Pallas kernels  73.2 us (98%)
  local copies, waits for them, and re-layouts  1.49 us (2%)
    pallas_call x1, Pallas kernels, layer(): pl.pallas_call(layer_kernel, out_shape=jax.ShapeDtypeStruct((4, 8192), BF...  73.2 us

profile of v11, /device:TPU:1, one launch (start us, length us, event | category | flops | bytes accessed | tf_op | source)
XLA Modules:
  0.0 74.7 jit_solution(7804320328681498484)
XLA Ops:
  0.0 73.2 %layer.1 = bf16[4,8192]{1,0:T(4,128)(2,1)} custom-call(bf16[4,8192]{1,0:T(4,128)(2,1)} %q_ref.1, bf16[512,1024]{1,0:T(8,128)(2,1)} %k_ref.1, bf16[512,1024]{1,0:T(8,128)(2,1)} %v_ref.1, bf16[256,512]{1,0:T(8,128)(2,1)} %w_ref.1, s32[64]{0:T(128)} %kinds_ref.1, s32[64]{0:T(128)} %counts_ref.1, s32[32,16,64]{2,1,0:T(8,128)} %bitcast.1, s32[64,1024]{1,0:T(8,128)} %cols_ref.1, ...), custom_call_target="tpu_custom_call" | custom-call | tf_op jit(solution)/shard_map/layer/pallas_call | solution.py:496
  73.2 1.5 %copy.11 = bf16[4,8192]{1,0:T(4,128)(2,1)} copy(bf16[4,8192]{1,0:T(4,128)(2,1)} %layer.1) | data formatting | bytes 131072

commit v12 on v11

--- a/solution.py
+++ b/solution.py
@@ -99,9 +99,9 @@
 
 def layer_kernel(
     q_ref, k_ref, v_ref, w_ref, kinds_ref, counts_ref, blocks_ref, cols_ref, offs_ref,
-    out_ref,
+    late, fr,
     qv, qt, qs, qy, q4, qf, qb, kl, kvb, wv, kind_ref, count_ref, blocks, cols8, offs8, row_bias, tile_bias,
-    top, total, mixed, o_out, st_out, ob, sb, share_of, ab, part, early, pieces, late, fb, fr,
+    top, total, mixed, o_out, st_out, ob, sb, share_of, ab, part, early, pieces, fb,
     in_sem, q1_send, q1_recv, q2_send, q2_recv, qx_send, qx_recv,
     kz_send, kz_recv, ky_send, ky_recv, kc_send, kc_recv,
     w_send, w_recv, wc_send, wc_recv, st_send, st_recv, ox_send, ox_recv,
@@ -479,14 +479,8 @@
             row_copy(j, d).wait_send()
     for copy in last:
         copy.wait_send()
-
     arrived(late, r_recv)
     arrived(fr, f_recv)
-    for tt in range(NT):
-        summed = fr[tt].astype(F32)
-        for e in range(4):
-            summed = summed + late[e, tt // 2, :, 512 * (tt % 2) : 512 * (tt % 2) + 512].astype(F32)
-        out_ref[:, 512 * tt : 512 * tt + 512] = summed.astype(BF16)
 
 
 def layer(q, k, v, w, kinds, counts, blocks, cols, offs):
@@ -495,9 +489,12 @@
     vmem = pltpu.VMEM
     return pl.pallas_call(
         layer_kernel,
-        out_shape=jax.ShapeDtypeStruct((4, 8192), BF16),
+        out_shape=(
+            jax.ShapeDtypeStruct((4, NY, 4, 1024), BF16),
+            jax.ShapeDtypeStruct((NT, 4, 512), BF16),
+        ),
         in_specs=[hbm] * 9,
-        out_specs=pl.BlockSpec(memory_space=pltpu.VMEM),
+        out_specs=(hbm, hbm),
         scratch_shapes=[
             vmem((4, 8192), BF16),
             vmem((KVH, NY, 4, HD), BF16),
@@ -528,8 +525,6 @@
             vmem((2, 2, 64, 512), BF16),
             vmem((4, 64, 512), BF16),
             vmem((2, NT, 4, 1024), BF16),
-            vmem((4, NY, 4, 1024), BF16),
-            vmem((NT, 4, 512), BF16),
             vmem((NT, 4, 512), BF16),
             dma((21,)),
             dma((8,)), dma, dma((16,)), dma, dma((4,)), dma((4,)),
@@ -545,7 +540,10 @@
 
 
 def shards(q, k, v, w, kinds, counts, blocks, cols, offs):
-    return layer(q, k, v, w, kinds, counts, blocks.transpose(1, 2, 0), cols, offs)
+    late, fr = layer(q, k, v, w, kinds, counts, blocks.transpose(1, 2, 0), cols, offs)
+    late = jnp.sum(late.astype(F32), axis=0).transpose(1, 0, 2).reshape(4, 8192)
+    fr = fr.transpose(1, 0, 2).reshape(4, 8192)
+    return (late + fr.astype(F32)).astype(BF16)
 
 
 def solution(mesh):

time: 74.9 us -> 75 us (level)
  other arithmetic: 0 us -> 1.81 us
  local copies, waits for them, and re-layouts: 1.49 us -> 0.01 us
    unnamed x1 -> x2, local copies, waits for them, and re-layouts: 1.49 us -> 0.01 us
    reduce_sum x0 -> x1, other arithmetic: none -> 1.13 us  [shards(): late = jnp.sum(late.astype(F32), axis=0).transpose(1, 0, 2).reshape(4, 8192)]
where the time goes in v12:
time: 75 us; the launch traced here: 74.9 us
  Pallas kernels  73 us (97%)
  other arithmetic  1.81 us (2%)
    pallas_call x1, Pallas kernels, layer(): pl.pallas_call(layer_kernel, out_shape=(jax.ShapeDtypeStruct((4, NY, 4, 1...  73 us

profile of v12, /device:TPU:1, one launch (start us, length us, event | category | flops | bytes accessed | tf_op | source)
XLA Modules:
  0.0 74.9 jit_solution(16898510462340831865)
XLA Ops:
  0.0 73.0 %layer.1 = (bf16[4,8,4,1024]{3,2,1,0:T(4,128)(2,1)}, bf16[16,4,512]{2,1,0:T(4,128)(2,1)}) custom-call(bf16[4,8192]{1,0:T(4,128)(2,1)} %q_ref.1, bf16[512,1024]{1,0:T(8,128)(2,1)} %k_ref.1, bf16[512,1024]{1,0:T(8,128)(2,1)} %v_ref.1, bf16[256,512]{1,0:T(8,128)(2,1)} %w_ref.1, s32[64]{0:T(128)} %kinds_ref.1, s32[64]{0:T(128)} %counts_ref.1, ...), custom_call_target="tpu_custom_call" | custom-call | tf_op jit(solution)/shard_map/layer/pallas_call | solution.py:490
  73.0 0.0 copy-start
  73.0 1.1 %convert_reduce_fusion = f32[8,4,1024]{2,1,0:T(4,128)S(1)} fusion(bf16[4,8,4,1024]{3,2,1,0:T(4,128)(2,1)} %get-tuple-element.7), kind=kLoop, calls=%fused_computation | loop fusion | flops 229376 | bytes 393216 | tf_op jit(solution)/shard_map/reduce_sum | solution.py:544
  74.2 0.0 copy-done
  74.2 0.7 add_convert_fusion
  (1 shorter events, 0.0 us)
Async XLA Ops:
  73.0 1.1 %copy-start = (bf16[16,4,512]{2,1,0:T(4,128)(2,1)S(1)}, bf16[16,4,512]{2,1,0:T(4,128)(2,1)}, u32[]{:S(2)}) copy-start(bf16[16,4,512]{2,1,0:T(4,128)(2,1)} %get-tuple-element.8) | copy-start | bytes 196612
